TPU v7x, 128 devices: a whole 4x4x4 slice. The times are simulated.
128 devices in a mesh: gx: 16 (over y, z), gy: 8 (over x, core).
Axes of the slice: x: 4, y: 4, z: 4, core: 2. Of those that a mesh axis runs over, the one named last changes fastest.
Arguments:
- points: float32 [65536, 768], P(('gx', 'gy'))
- labels: float32 [65536, 64], P(('gx', 'gy')), may hold values from -16 to 16
- skeleton_rows: int32 [128, 256], P(('gx', 'gy')), may hold values from 0 to 511, as said below
- upper_rows: int32 [16, 256], P('gx'), may hold values from 0 to 2047, as said below
- near_list: int32 [256, 8], P(('gx', 'gy')), may hold values from 0 to 255, as said below
- far_local: int32 [128, 7], P(('gx', 'gy')), may hold values from -1 to 7, as said below
- far_upper: int32 [128, 15], P(('gx', 'gy')), may hold values from -1 to 15, as said below
Outputs:
- propagated: float32 [65536, 64], P(('gx', 'gy'))
Inputs may be any that keep to these rules, and one draw needn't show every extreme that they name: `skeleton_rows`: entries of one row are distinct. `upper_rows`: entries of one row are distinct. `near_list`: row l lists distinct leaves of l's own outer cluster; its first entry is l itself. `far_local`: row g lists distinct node numbers within g's outer cluster (0 to 7), never g's own, first, then -1 in the remaining slots; at least one entry; some node lists all 7 others. `far_upper`: row g lists distinct outer clusters, never g's own, first, then -1 in the remaining slots; at least one entry; some node lists all 15 others.
All inputs are finite; a program needn't handle non-finite values.
Results may differ from a plain program's by a relative error of at most 0.0003.
Values sent between devices are 32-bit elements; how exact they have to be, the bound alone decides.
A program may use at most 128 MiB of HBM per device.

v0:
```python
import jax
import jax.numpy as jnp
from jax import lax
from jax.sharding import PartitionSpec as P

LEAF = 256


kernel_scale = 0.04
highest = lax.Precision.HIGHEST


def affinity(left_rows, right_rows):
    cross = jnp.einsum(
        "id,jd->ij", left_rows, right_rows, precision=highest, preferred_element_type=jnp.float32
    )
    left_sq = jnp.sum(left_rows * left_rows, axis=1)
    right_sq = jnp.sum(right_rows * right_rows, axis=1)
    return jnp.exp((2.0 * cross - left_sq[:, None] - right_sq[None, :]) / kernel_scale)


def product(left_rows, right_rows):
    return jnp.dot(left_rows, right_rows, precision=highest, preferred_element_type=jnp.float32)


def compress_with(affine, member_labels, member_mass, totals):
    shares = affine / totals[None, :]
    return (product(shares, member_labels), product(shares, member_mass))


def masked_terms(targets, sources, source_weights, source_mass, keep_cols):
    weight = jnp.where(keep_cols[None, :], affinity(targets, sources), 0.0)
    return (product(weight, source_weights), product(weight, source_mass))


def on_device(points, labels, skeleton_rows, upper_rows, near_list, far_local, far_upper):
    row_count = points.shape[0]
    width = points.shape[1]
    label_width = labels.shape[1]
    leaf_dev = row_count // LEAF
    skeleton_size = skeleton_rows.shape[1]
    n_gy = lax.axis_size("gy")
    outer_index = lax.axis_index("gx")
    inner_index = lax.axis_index("gy")
    first_leaf = outer_index * n_gy * leaf_dev
    lower_points = jnp.take(points, skeleton_rows[0], axis=0)
    lower_aff = affinity(lower_points, points)
    lower_weights, lower_mass = compress_with(
        lower_aff, labels, jnp.ones((row_count,), jnp.float32), jnp.sum(lower_aff, axis=0)
    )
    targets = points.reshape(leaf_dev, LEAF, width)
    target_rows = (inner_index * row_count + jnp.arange(row_count, dtype=jnp.int32)).reshape(
        leaf_dev, LEAF
    )
    sources = lax.all_gather(points, "gy", axis=0, tiled=True)
    source_labels = lax.all_gather(labels, "gy", axis=0, tiled=True)
    piece_rows = sources.shape[0]

    def per_leaf(leaf_items):
        target_block, listed, block_rows = leaf_items

        def visit(running, source_leaf):
            start = (source_leaf - first_leaf) * LEAF

            def add_tile(current):
                begin = jnp.clip(start, 0, piece_rows - LEAF)
                tile_points = lax.dynamic_slice_in_dim(sources, begin, LEAF, 0)
                tile_labels = lax.dynamic_slice_in_dim(source_labels, begin, LEAF, 0)
                columns = begin + jnp.arange(LEAF, dtype=jnp.int32)
                owned = first_leaf + columns // LEAF == source_leaf
                allowed = owned[None, :] & (block_rows[:, None] != columns[None, :])
                weight = jnp.where(allowed, affinity(target_block, tile_points), 0.0)
                return (
                    current[0] + product(weight, tile_labels),
                    current[1] + jnp.sum(weight, axis=1),
                )

            inside = (start < piece_rows) & (start + LEAF > 0)
            return (lax.cond(inside, add_tile, lambda current: current, running), None)

        zero_pair = (jnp.zeros((LEAF, label_width), jnp.float32), jnp.zeros((LEAF,), jnp.float32))
        result, _ = lax.scan(visit, zero_pair, listed)
        return result

    leaf_sums, leaf_counts = lax.map(per_leaf, (targets, near_list, target_rows))
    child_points, child_weights, child_mass = (
        lax.all_gather(lower_points, "gy", axis=0, tiled=True),
        lax.all_gather(lower_weights, "gy", axis=0, tiled=True),
        lax.all_gather(lower_mass, "gy", axis=0, tiled=True),
    )
    child_owner = jnp.arange(child_points.shape[0], dtype=jnp.int32) // skeleton_size
    keep_local = jnp.any(far_local[0][:, None] == child_owner[None, :], axis=0)
    local_sum, local_count = masked_terms(
        points, child_points, child_weights, child_mass, keep_local
    )
    listed_groups = far_upper[0]
    far_start = (
        jnp.zeros((row_count, label_width), jnp.float32),
        jnp.zeros((row_count,), jnp.float32),
    )
    whole_points = jnp.take(child_points, upper_rows[0], axis=0)
    whole_aff = affinity(whole_points, child_points)
    whole_weights, whole_mass = compress_with(
        whole_aff, child_weights, child_mass, jnp.sum(whole_aff, axis=0)
    )
    far_sources = lax.all_gather(whole_points, "gx", axis=0, tiled=True)
    source_weights = lax.all_gather(whole_weights, "gx", axis=0, tiled=True)
    source_mass = lax.all_gather(whole_mass, "gx", axis=0, tiled=True)
    far_piece_rows = far_sources.shape[0]
    column_group = jnp.arange(far_piece_rows, dtype=jnp.int32) // skeleton_size
    keep_cols = jnp.any(listed_groups[:, None] == column_group[None, :], axis=0)
    blocks = far_piece_rows // skeleton_size

    def add_block(partial_value, block_items):
        part_points, part_weights, part_mass, part_keep = block_items
        add_sum, add_count = masked_terms(points, part_points, part_weights, part_mass, part_keep)
        return ((partial_value[0] + add_sum, partial_value[1] + add_count), None)

    result, _ = lax.scan(
        add_block,
        far_start,
        (
            far_sources.reshape(blocks, skeleton_size, width),
            source_weights.reshape(blocks, skeleton_size, label_width),
            source_mass.reshape(blocks, skeleton_size),
            keep_cols.reshape(blocks, skeleton_size),
        ),
    )
    upper_sum, upper_count = result
    numerator = leaf_sums.reshape(row_count, label_width) + local_sum + upper_sum
    denominator = leaf_counts.reshape(row_count) + local_count + upper_count
    return numerator / denominator[:, None]


def solution(mesh):
    return jax.shard_map(
        on_device,
        mesh=mesh,
        in_specs=(
            P(("gx", "gy"), None),
            P(("gx", "gy"), None),
            P(("gx", "gy"), None),
            P("gx", None),
            P(("gx", "gy"), None),
            P(("gx", "gy"), None),
            P(("gx", "gy"), None),
        ),
        out_specs=P(("gx", "gy"), None),
        check_vma=False,
    )
```

profile of v0, /device:TPU:1, one launch (start us, length us, event | category | flops | bytes accessed | tf_op | source)
XLA Modules:
  0.0 433.0 jit_solution(3465733435029998676)
XLA Ops:
  16.0 15.4 %all_gather.27 = f32[2048,64]{0,1:T(8,128)S(1)} all-gather(f32[256,64]{0,1:T(8,128)S(1)} %fusion.41), channel_id=1, replica_groups=mesh['gx'=16,'gy'=8] {'gy'}, dimensions={0}, use_global_device_ids=true | all-gather | bytes 589824 | tf_op jit(solution)/shard_map/all_gather | solution.py:88
  31.4 25.4 %all-gather.12.cloned.1.call-done = f32[2048,768]{1,0:T(8,128)} async-done(((f32[256,768]{1,0:T(8,128)}), f32[2048,768]{1,0:T(8,128)}) %all-gather.12.cloned.1.call-update) | async-done | bytes 6291472 | tf_op jit(solution)/shard_map/all_gather | solution.py:87
  56.8 4.2 gather_fusion.1
  61.2 3.6 multiply_reduce_fusion.2
  64.8 7.8 %fusion.52 = (f32[2048]{0:T(1024)S(1)}, f32[256,2048]{1,0:T(8,128)S(1)}) fusion(f32[2048]{0:T(1024)S(1)} %multiply_reduce_fusion.2, f32[256]{0:T(256)S(1)} %get-tuple-element.358, f32[256,768]{1,0:T(8,128)S(1)} %get-tuple-element.359, f32[2048,768]{1,0:T(8,128)} %all-gather.12.cloned.1.call-done), kind=kOutput, calls=%fused_computation.107 | convolution fusion | flops 4834457600 | bytes 9192448 | tf_op jit(solution)/shard_map/id,jd->ij/dot_general | solution.py:14
  79.4 8.9 %all-gather = f32[8,1,256]{2,1,0:T(1,128)S(1)} all-gather(f32[1,1,256]{2,1,0:T(1,128)S(1)} %convolution_bitcast_fusion), channel_id=1, replica_groups=mesh['gx'=16,'gy'=8] {'gy'}, dimensions={0}, use_global_device_ids=true | all-gather | bytes 9216 | tf_op jit(solution)/shard_map/all_gather | solution.py:89
  88.4 3.4 convolution_bitcast_fusion.1
  91.9 18.7 %all-gather.1 = f32[16,1,256]{2,1,0:T(1,128)S(1)} all-gather(f32[1,1,256]{2,1,0:T(1,128)S(1)} %convolution_bitcast_fusion.1), channel_id=1, replica_groups=mesh['gx'=16,'gy'=8] {'gx'}, dimensions={0}, use_global_device_ids=true | all-gather | bytes 17408 | tf_op jit(solution)/shard_map/all_gather | solution.py:108
  110.6 12.8 %exponential_select_fusion = f32[2048,512]{1,0:T(8,128)S(1)} fusion(f32[2048,768]{1,0:T(8,128)} %all-gather.12.cloned.1.call-done, f32[512,768]{1,0:T(8,128)S(1)} %copy-done.1, f32[2048]{0:T(1024)S(1)} %multiply_reduce_fusion.2, f32[512]{0:T(512)S(1)} %multiply_reduce_fusion.3, pred[2048]{0:T(1024)(128)(4,1)S(1)} %compare_reduce_fusion.1), kind=kOutput, calls=%fused_computation.51 | convolution fusion | flops 9668919296 | bytes 12070912 | tf_op jit(solution)/shard_map/id,jd->ij/dot_general | solution.py:14
  130.8 15.6 %all-gather.10.cloned.1.call-done = f32[4096,64]{1,0:T(8,128)} async-done(((f32[512,64]{1,0:T(8,128)}), f32[4096,64]{1,0:T(8,128)}) %all-gather.10.cloned.1.call-update) | async-done | bytes 1048592 | tf_op jit(solution)/shard_map/all_gather | solution.py:56
  146.4 69.2 %all-gather.8.cloned.1.call-done = f32[4096,768]{1,0:T(8,128)} async-done(((f32[512,768]{1,0:T(8,128)}), f32[4096,768]{1,0:T(8,128)}) %all-gather.8.cloned.1.call-update) | async-done | bytes 12582928 | tf_op jit(solution)/shard_map/all_gather | solution.py:55
  215.6 112.6 %while.40 = (s32[]{:T(128)}, f32[2,256,64]{1,0,2:T(2,128)S(1)}, f32[2,256]{1,0:T(2,128)S(1)}, s32[2,8]{1,0:T(2,128)S(1)}, s32[2,256]{1,0:T(2,128)S(1)}, /*index=...) while((s32[]{:T(128)}, f32[2,256,64]{1,0,2:T(2,128)S(1)}, ...), condition=%wide.region_8.9_spmd, body=%wide.region_0.8_spmd.sunk | while | flops 655642880 | bytes 5850316 | solution.py:85
  215.8 55.3 %while.42 = (s32[]{:T(128)}, f32[256,64]{0,1:T(8,128)S(1)}, f32[256]{0:T(256)S(1)}, s32[8]{0:T(128)S(1)}, s32[]{:T(128)}, /*index=5*/s32[256]{0:T(256)S(1)}, f32...) while((s32[]{:T(128)}, f32[256,64]{0,1:T(8,128)S(1)}, ...), condition=%wide.region_7.7_spmd, body=%wide.region_1.6_spmd.sunk | while | flops 655642880 | bytes 3944299 | solution.py:82
  217.1 5.5 %conditional.2 = ((f32[256,64]{0,1:T(8,128)S(1)}, f32[256]{0:T(256)S(1)})) conditional(s32[]{:T(128)} %convert_element_type.4, (f32[256,64]{0,1:T(8,128)S(1)}, f32[256]{0:T(256)S(1)}) %tuple.77, (s32[]{:T(128)}, s32[]{:T(128)}, s32[]{:T(128)}, s32[256]{0:T(256)S(1)}, f32[4096,768]{1,0:T(8,128)}, /*index=5*/f32[256,768]{1,0:T(8,128)S(1)}, ...), branch_computations={%region_2.1_spmd, %region_3.5_spmd} | conditional | flops 655642880 | bytes 3944012 | solution.py:79
  224.0 5.6 %conditional.2 = ((f32[256,64]{0,1:T(8,128)S(1)}, f32[256]{0:T(256)S(1)})) conditional(s32[]{:T(128)} %convert_element_type.4, (f32[256,64]{0,1:T(8,128)S(1)}, f32[256]{0:T(256)S(1)}) %tuple.77, (s32[]{:T(128)}, s32[]{:T(128)}, s32[]{:T(128)}, s32[256]{0:T(256)S(1)}, f32[4096,768]{1,0:T(8,128)}, /*index=5*/f32[256,768]{1,0:T(8,128)S(1)}, ...), branch_computations={%region_2.1_spmd, %region_3.5_spmd} | conditional | flops 655642880 | bytes 3944012 | solution.py:79
  230.9 5.5 %conditional.2 = ((f32[256,64]{0,1:T(8,128)S(1)}, f32[256]{0:T(256)S(1)})) conditional(s32[]{:T(128)} %convert_element_type.4, (f32[256,64]{0,1:T(8,128)S(1)}, f32[256]{0:T(256)S(1)}) %tuple.77, (s32[]{:T(128)}, s32[]{:T(128)}, s32[]{:T(128)}, s32[256]{0:T(256)S(1)}, f32[4096,768]{1,0:T(8,128)}, /*index=5*/f32[256,768]{1,0:T(8,128)S(1)}, ...), branch_computations={%region_2.1_spmd, %region_3.5_spmd} | conditional | flops 655642880 | bytes 3944012 | solution.py:79
  237.8 5.5 %conditional.2 = ((f32[256,64]{0,1:T(8,128)S(1)}, f32[256]{0:T(256)S(1)})) conditional(s32[]{:T(128)} %convert_element_type.4, (f32[256,64]{0,1:T(8,128)S(1)}, f32[256]{0:T(256)S(1)}) %tuple.77, (s32[]{:T(128)}, s32[]{:T(128)}, s32[]{:T(128)}, s32[256]{0:T(256)S(1)}, f32[4096,768]{1,0:T(8,128)}, /*index=5*/f32[256,768]{1,0:T(8,128)S(1)}, ...), branch_computations={%region_2.1_spmd, %region_3.5_spmd} | conditional | flops 655642880 | bytes 3944012 | solution.py:79
  244.7 5.5 %conditional.2 = ((f32[256,64]{0,1:T(8,128)S(1)}, f32[256]{0:T(256)S(1)})) conditional(s32[]{:T(128)} %convert_element_type.4, (f32[256,64]{0,1:T(8,128)S(1)}, f32[256]{0:T(256)S(1)}) %tuple.77, (s32[]{:T(128)}, s32[]{:T(128)}, s32[]{:T(128)}, s32[256]{0:T(256)S(1)}, f32[4096,768]{1,0:T(8,128)}, /*index=5*/f32[256,768]{1,0:T(8,128)S(1)}, ...), branch_computations={%region_2.1_spmd, %region_3.5_spmd} | conditional | flops 655642880 | bytes 3944012 | solution.py:79
  251.6 5.7 %conditional.2 = ((f32[256,64]{0,1:T(8,128)S(1)}, f32[256]{0:T(256)S(1)})) conditional(s32[]{:T(128)} %convert_element_type.4, (f32[256,64]{0,1:T(8,128)S(1)}, f32[256]{0:T(256)S(1)}) %tuple.77, (s32[]{:T(128)}, s32[]{:T(128)}, s32[]{:T(128)}, s32[256]{0:T(256)S(1)}, f32[4096,768]{1,0:T(8,128)}, /*index=5*/f32[256,768]{1,0:T(8,128)S(1)}, ...), branch_computations={%region_2.1_spmd, %region_3.5_spmd} | conditional | flops 655642880 | bytes 3944012 | solution.py:79
  258.7 5.5 %conditional.2 = ((f32[256,64]{0,1:T(8,128)S(1)}, f32[256]{0:T(256)S(1)})) conditional(s32[]{:T(128)} %convert_element_type.4, (f32[256,64]{0,1:T(8,128)S(1)}, f32[256]{0:T(256)S(1)}) %tuple.77, (s32[]{:T(128)}, s32[]{:T(128)}, s32[]{:T(128)}, s32[256]{0:T(256)S(1)}, f32[4096,768]{1,0:T(8,128)}, /*index=5*/f32[256,768]{1,0:T(8,128)S(1)}, ...), branch_computations={%region_2.1_spmd, %region_3.5_spmd} | conditional | flops 655642880 | bytes 3944012 | solution.py:79
  265.5 5.5 %conditional.2 = ((f32[256,64]{0,1:T(8,128)S(1)}, f32[256]{0:T(256)S(1)})) conditional(s32[]{:T(128)} %convert_element_type.4, (f32[256,64]{0,1:T(8,128)S(1)}, f32[256]{0:T(256)S(1)}) %tuple.77, (s32[]{:T(128)}, s32[]{:T(128)}, s32[]{:T(128)}, s32[256]{0:T(256)S(1)}, f32[4096,768]{1,0:T(8,128)}, /*index=5*/f32[256,768]{1,0:T(8,128)S(1)}, ...), branch_computations={%region_2.1_spmd, %region_3.5_spmd} | conditional | flops 655642880 | bytes 3944012 | solution.py:79
  272.2 55.0 %while.42 = (s32[]{:T(128)}, f32[256,64]{0,1:T(8,128)S(1)}, f32[256]{0:T(256)S(1)}, s32[8]{0:T(128)S(1)}, s32[]{:T(128)}, /*index=5*/s32[256]{0:T(256)S(1)}, f32...) while((s32[]{:T(128)}, f32[256,64]{0,1:T(8,128)S(1)}, ...), condition=%wide.region_7.7_spmd, body=%wide.region_1.6_spmd.sunk | while | flops 655642880 | bytes 3944299 | solution.py:82
  273.6 5.5 %conditional.2 = ((f32[256,64]{0,1:T(8,128)S(1)}, f32[256]{0:T(256)S(1)})) conditional(s32[]{:T(128)} %convert_element_type.4, (f32[256,64]{0,1:T(8,128)S(1)}, f32[256]{0:T(256)S(1)}) %tuple.77, (s32[]{:T(128)}, s32[]{:T(128)}, s32[]{:T(128)}, s32[256]{0:T(256)S(1)}, f32[4096,768]{1,0:T(8,128)}, /*index=5*/f32[256,768]{1,0:T(8,128)S(1)}, ...), branch_computations={%region_2.1_spmd, %region_3.5_spmd} | conditional | flops 655642880 | bytes 3944012 | solution.py:79
  280.5 5.5 %conditional.2 = ((f32[256,64]{0,1:T(8,128)S(1)}, f32[256]{0:T(256)S(1)})) conditional(s32[]{:T(128)} %convert_element_type.4, (f32[256,64]{0,1:T(8,128)S(1)}, f32[256]{0:T(256)S(1)}) %tuple.77, (s32[]{:T(128)}, s32[]{:T(128)}, s32[]{:T(128)}, s32[256]{0:T(256)S(1)}, f32[4096,768]{1,0:T(8,128)}, /*index=5*/f32[256,768]{1,0:T(8,128)S(1)}, ...), branch_computations={%region_2.1_spmd, %region_3.5_spmd} | conditional | flops 655642880 | bytes 3944012 | solution.py:79
  287.4 5.5 %conditional.2 = ((f32[256,64]{0,1:T(8,128)S(1)}, f32[256]{0:T(256)S(1)})) conditional(s32[]{:T(128)} %convert_element_type.4, (f32[256,64]{0,1:T(8,128)S(1)}, f32[256]{0:T(256)S(1)}) %tuple.77, (s32[]{:T(128)}, s32[]{:T(128)}, s32[]{:T(128)}, s32[256]{0:T(256)S(1)}, f32[4096,768]{1,0:T(8,128)}, /*index=5*/f32[256,768]{1,0:T(8,128)S(1)}, ...), branch_computations={%region_2.1_spmd, %region_3.5_spmd} | conditional | flops 655642880 | bytes 3944012 | solution.py:79
  294.3 5.5 %conditional.2 = ((f32[256,64]{0,1:T(8,128)S(1)}, f32[256]{0:T(256)S(1)})) conditional(s32[]{:T(128)} %convert_element_type.4, (f32[256,64]{0,1:T(8,128)S(1)}, f32[256]{0:T(256)S(1)}) %tuple.77, (s32[]{:T(128)}, s32[]{:T(128)}, s32[]{:T(128)}, s32[256]{0:T(256)S(1)}, f32[4096,768]{1,0:T(8,128)}, /*index=5*/f32[256,768]{1,0:T(8,128)S(1)}, ...), branch_computations={%region_2.1_spmd, %region_3.5_spmd} | conditional | flops 655642880 | bytes 3944012 | solution.py:79
  301.1 5.5 %conditional.2 = ((f32[256,64]{0,1:T(8,128)S(1)}, f32[256]{0:T(256)S(1)})) conditional(s32[]{:T(128)} %convert_element_type.4, (f32[256,64]{0,1:T(8,128)S(1)}, f32[256]{0:T(256)S(1)}) %tuple.77, (s32[]{:T(128)}, s32[]{:T(128)}, s32[]{:T(128)}, s32[256]{0:T(256)S(1)}, f32[4096,768]{1,0:T(8,128)}, /*index=5*/f32[256,768]{1,0:T(8,128)S(1)}, ...), branch_computations={%region_2.1_spmd, %region_3.5_spmd} | conditional | flops 655642880 | bytes 3944012 | solution.py:79
  308.0 5.5 %conditional.2 = ((f32[256,64]{0,1:T(8,128)S(1)}, f32[256]{0:T(256)S(1)})) conditional(s32[]{:T(128)} %convert_element_type.4, (f32[256,64]{0,1:T(8,128)S(1)}, f32[256]{0:T(256)S(1)}) %tuple.77, (s32[]{:T(128)}, s32[]{:T(128)}, s32[]{:T(128)}, s32[256]{0:T(256)S(1)}, f32[4096,768]{1,0:T(8,128)}, /*index=5*/f32[256,768]{1,0:T(8,128)S(1)}, ...), branch_computations={%region_2.1_spmd, %region_3.5_spmd} | conditional | flops 655642880 | bytes 3944012 | solution.py:79
  314.8 5.5 %conditional.2 = ((f32[256,64]{0,1:T(8,128)S(1)}, f32[256]{0:T(256)S(1)})) conditional(s32[]{:T(128)} %convert_element_type.4, (f32[256,64]{0,1:T(8,128)S(1)}, f32[256]{0:T(256)S(1)}) %tuple.77, (s32[]{:T(128)}, s32[]{:T(128)}, s32[]{:T(128)}, s32[256]{0:T(256)S(1)}, f32[4096,768]{1,0:T(8,128)}, /*index=5*/f32[256,768]{1,0:T(8,128)S(1)}, ...), branch_computations={%region_2.1_spmd, %region_3.5_spmd} | conditional | flops 655642880 | bytes 3944012 | solution.py:79
  321.7 5.5 %conditional.2 = ((f32[256,64]{0,1:T(8,128)S(1)}, f32[256]{0:T(256)S(1)})) conditional(s32[]{:T(128)} %convert_element_type.4, (f32[256,64]{0,1:T(8,128)S(1)}, f32[256]{0:T(256)S(1)}) %tuple.77, (s32[]{:T(128)}, s32[]{:T(128)}, s32[]{:T(128)}, s32[256]{0:T(256)S(1)}, f32[4096,768]{1,0:T(8,128)}, /*index=5*/f32[256,768]{1,0:T(8,128)S(1)}, ...), branch_computations={%region_2.1_spmd, %region_3.5_spmd} | conditional | flops 655642880 | bytes 3944012 | solution.py:79
  328.3 92.5 %while.41 = (s32[]{:T(128)}, f32[512,64]{0,1:T(8,128)S(1)}, f32[512]{0:T(512)S(1)}, pred[16,256]{1,0:T(8,128)(4,1)S(1)}, f32[16,256,768]{2,1,0:T(8,128)}, /*inde...) while((s32[]{:T(128)}, f32[512,64]{0,1:T(8,128)S(1)}, ...), condition=%wide.region_19.20_spmd.clone, body=%wide.region_17.19_spmd.clone.sunk | while | flops 1311310592 | bytes 5127044 | solution.py:119
  420.8 5.6 %fusion.39 = f32[512,64]{0,1:T(8,128)} fusion(f32[512,64]{0,1:T(8,128)S(1)} %get-tuple-element.235, f32[512,64]{0,1:T(8,128)S(1)} %bitcast.118, f32[2048,512]{1,0:T(8,128)} %copy-done.2, f32[2048,64]{0,1:T(8,128)S(1)} %all_gather.27, f32[512]{0:T(512)S(1)} %add_add_fusion), kind=kOutput, calls=%fused_computation.65 | convolution fusion | flops 805404672 | bytes 5113856 | tf_op jit(solution)/shard_map/dot_general | solution.py:23
  (293 shorter events, 216.3 us)
Async XLA Ops:
  6.5 50.3 %all-gather.12.cloned.1.call-start = ((), (), s32[]{:S(2)}) async-start(), calls=%async_computation.2 | async-start | bytes 7077888 | tf_op jit(solution)/shard_map/all_gather | solution.py:87
  10.7 1.1 copy-start.9
  10.7 1.7 copy-start
  11.8 1.3 copy-start.4
  11.8 115.8 %all-gather.16.cloned.1.call-start = ((), (), s32[]{:S(2)}) async-start(), calls=%async_computation.4 | async-start | bytes 1114112 | tf_op jit(solution)/shard_map/all_gather | solution.py:107
  12.4 3.0 copy-start.8
  14.6 0.8 copy-start.6
  61.2 3.6 copy-start.3
  72.6 1.3 copy-start.5
  76.6 2.2 copy-start.11
  76.6 2.3 copy-start.7
  76.6 69.9 %all-gather.10.cloned.1.call-start = ((), (), s32[]{:S(2)}) async-start(), calls=%async_computation.1 | async-start | bytes 2359296 | tf_op jit(solution)/shard_map/all_gather | solution.py:56
  77.5 10.8 %copy-start.10 = (s32[1,7]{1,0:T(1,128)S(1)}, s32[1,7]{1,0:T(1,128)}, u32[]{:S(2)}) copy-start(s32[1,7]{1,0:T(1,128)} %param.20) | copy-start | bytes 88
  77.5 138.1 %all-gather.8.cloned.1.call-start = ((), (), s32[]{:S(2)}) async-start(), calls=%async_computation | async-start | bytes 14155776 | tf_op jit(solution)/shard_map/all_gather | solution.py:55
  78.1 250.2 %all-gather.14.cloned.1.call-start = ((), (), s32[]{:S(2)}) async-start(), calls=%async_computation.3 | async-start | bytes 13369344 | tf_op jit(solution)/shard_map/all_gather | solution.py:106
  88.4 22.2 %copy-start.1 = (f32[512,768]{1,0:T(8,128)S(1)}, f32[512,768]{1,0:T(8,128)}, u32[]{:S(2)}) copy-start(f32[512,768]{1,0:T(8,128)} %param.15) | copy-start | bytes 4718596
  123.4 2.0 copy-start.2
  127.6 88.0 %copy-start.12 = (s32[2,8]{1,0:T(2,128)S(1)}, s32[2,8]{1,0:T(2,128)}, u32[]{:S(2)}) copy-start(s32[2,8]{1,0:T(2,128)} %param.19) | copy-start | bytes 196
Sparse Core Ops, SparseCore 0:
  11.9 44.8 all-gather.11
  76.7 41.7 all-gather.15
  120.3 26.1 all-gather.9
  148.0 67.6 all-gather.7
  217.7 90.0 all-gather.13
where the time goes:
time: 437 us; the launch traced here: 433 us
  matrix products  163 us (37%)
  waiting for transfers between devices  111 us (25%)
  other arithmetic  60.5 us (14%)
  blocking collectives  43 us (10%)
  local copies, waits for them, and re-layouts  29.2 us (7%)
  between operations  13.4 us (3%)
  loops' own time  12.8 us (3%)
    dot_general x35, matrix products, affinity(): jnp.einsum('id,jd->ij', left_rows, right_rows, precision=highest, preferr...  99 us
    all_gather x1, waiting for transfers between devices, on_device(): sources = lax.all_gather(points, 'gy', axis=0, tiled=True)  69.2 us
    dot_general x54, matrix products, product(): jnp.dot(left_rows, right_rows, precision=highest, preferred_element_type=...  63.6 us
    reduce_sum x33, other arithmetic, affinity(): right_sq = jnp.sum(right_rows * right_rows, axis=1)  46 us
    all_gather x1, waiting for transfers between devices, on_device(): lax.all_gather(lower_points, 'gy', axis=0, tiled=True)  25.4 us
    all_gather x1, blocking collectives, on_device(): source_mass = lax.all_gather(whole_mass, 'gx', axis=0, tiled=True)  18.7 us
    all_gather x1, waiting for transfers between devices, on_device(): source_labels = lax.all_gather(labels, 'gy', axis=0, tiled=True)  15.6 us
    all_gather x1, blocking collectives, on_device(): lax.all_gather(lower_weights, 'gy', axis=0, tiled=True)  15.4 us
  transfers between devices with their start and end apart: 5, of which 3 were waited for; matrix products, arithmetic and copies ran while one was open for 29% of the time, Pallas kernels for 0%

commit v1 on v0

v1 whole, which is shorter than its diff:
```python
import functools
import math

import jax
import jax.numpy as jnp
from jax import lax
from jax.experimental import pallas as pl
from jax.experimental.pallas import tpu as pltpu
from jax.sharding import PartitionSpec as P

MESH = pl.DeviceIdType.MESH
F32, BF16 = jnp.float32, jnp.bfloat16
ROWS, WIDTH, LABELS, SKEL, LEAF = 512, 768, 64, 256, 256
MSG = 72
CHUNKS = 8
CHUNK = ROWS // CHUNKS
BETA = 25.0 * math.log2(math.e)


def dot_nt(a, b):
    return lax.dot_general(a, b, (((1,), (1,)), ((), ())), preferred_element_type=F32)


def dot_nn(a, b):
    return jnp.dot(a, b, preferred_element_type=F32)


def split(value):
    high = value.astype(BF16)
    return high, (value - high.astype(F32)).astype(BF16)


def kernel(x_ref, lab_ref, skel_ref, urow_ref, near_ref, flocal_ref, fupper_ref, out_ref,
           pts, hi, lo, ncol, nrow, rt, masks, kown, scol, srow,
           contr, contr_in, part, land1, mid, land2, uq, uhi, ulo, uncol,
           up, uphi, uplo, upnrow,
           wp, wp_in, wpart, wland1, wmid, wland2, upw,
           acc, ret_out, ret_in,
           own_sem, s_sem, r_sem):
    gx, gy = lax.axis_index("gx"), lax.axis_index("gy")
    c, j = lax.div(gy, 2), lax.rem(gy, 2)
    y, z = lax.div(gx, 4), lax.rem(gx, 4)
    half = lax.div(c, 2)
    other = 1 - j
    crossed = lax.rem(j + half, 2)
    before, after = lax.rem(c + 3, 4), lax.rem(c + 1, 4)

    def chip(step, core):
        return (gx, lax.rem(c + step, 4) * 2 + core)

    sib = (gx, c * 2 + other)

    def y_peer(step):
        return (lax.rem(y + step, 4) * 4 + z, gy)

    def z_peer(step):
        return (y * 4 + lax.rem(z + step, 4), gy)

    partners = [sib] + [chip(s, k) for s in (1, 3) for k in (j, other)]
    partners += [y_peer(s) for s in (1, 2, 3)] + [z_peer(s) for s in (1, 2, 3)]
    barrier = pltpu.get_barrier_semaphore()
    for partner in partners:
        pl.semaphore_signal(barrier, inc=1, device_id=partner, device_id_type=MESH)
    pl.semaphore_wait(barrier, len(partners))

    started = []

    def send(src, dst, device):
        at = len(started)
        copy = pltpu.make_async_remote_copy(
            src_ref=src, dst_ref=dst, send_sem=s_sem.at[at], recv_sem=r_sem.at[at],
            device_id=device, device_id_type=MESH)
        copy.start()
        started.append(copy)
        return copy

    nodes = [gy, c * 2 + other, before * 2 + j, before * 2 + other, after * 2 + j, after * 2 + other]
    cross_slot, cross_node = 4 + half, after * 2 + crossed

    bulk = {}

    def send_bulk(at):
        rows = pl.ds(at * CHUNK, CHUNK)
        bulk[1, at] = send(x_ref.at[rows], pts.at[2, rows], chip(1, j))
        bulk[3, at] = send(x_ref.at[rows], pts.at[4, rows], chip(3, j))

    own_copy = pltpu.make_async_copy(x_ref, pts.at[0], own_sem)
    own_copy.start()
    send_bulk(0)
    sib_points = send(x_ref, pts.at[1], sib)

    def prep(slot, leaf):
        def body(i, carry):
            rows = pl.ds(pl.multiple_of(leaf * 256 + i * 128, 128), 128)
            value = pts[slot, rows, :]
            high, low = split(value)
            hi[slot, rows, :] = high
            lo[slot, rows, :] = low
            norm = jnp.sum(value * value, axis=1, keepdims=True) * BETA
            wide = jnp.broadcast_to(norm, (128, 128))
            ncol[slot, rows, :] = wide
            nrow[slot, :, rows] = jnp.transpose(wide)[0:8, :]
            return carry
        lax.fori_loop(0, 2, body, 0)

    def affine(t_hi, t_lo, t_col, s_hi, s_lo, s_row):
        cross = dot_nt(t_hi, s_hi) + dot_nt(t_hi, s_lo) + dot_nt(t_lo, s_hi)
        return jnp.exp2(cross * (2.0 * BETA) - jnp.concatenate([t_col, t_col], axis=1) - s_row)

    def product_nt(k, rhs):
        k_hi, k_lo = split(k)
        r_hi, r_lo = split(rhs)
        both = dot_nt(k_hi, jnp.concatenate([r_hi, r_lo], axis=0))
        return both[:, :128] + both[:, 128:] + dot_nt(k_lo, r_hi)

    def product_nn(k, rhs):
        k_hi, k_lo = split(k)
        r_hi, r_lo = split(rhs)
        both = dot_nn(k_hi, jnp.concatenate([r_hi, r_lo], axis=1))
        return both[:, :128] + both[:, 128:] + dot_nn(k_lo, r_hi)

    def leaf_rows(leaf):
        return pl.ds(pl.multiple_of(leaf * 256, 256), 256)

    def block_affine(tb, t, sb, s):
        tr, sr = leaf_rows(t), leaf_rows(s)
        return affine(hi[tb, tr, :], lo[tb, tr, :], ncol[tb, tr, :],
                      hi[sb, sr, :], lo[sb, sr, :], nrow[sb, 0:1, sr])

    lane = lax.broadcasted_iota(jnp.int32, (1, 128), 1)

    def pick(tb, row, at):
        return jnp.sum(jnp.where(lane == at, masks[tb, pl.ds(row, 1), :], 0.0), axis=1, keepdims=True)

    def add_terms(k, tb, t, sb, s, node, target):
        sr = leaf_rows(s)
        rhs = pick(tb, t, 2 * node + s) * rt[sb, 0, :, sr] + pick(tb, 2, node) * rt[sb, 1, :, sr]
        tr = leaf_rows(t)
        acc[target, tr, :] += product_nt(k, rhs)

    def near(tb, sb, s, node, target):
        def body(t, carry):
            add_terms(block_affine(tb, t, sb, s), tb, t, sb, s, node, target)
            return carry
        lax.fori_loop(0, 2, body, 0)

    def far(tb, target, first, count):
        def body(i, carry):
            f = first + lax.div(i, 2)
            t = lax.rem(i, 2)
            q, yy = lax.div(f, 4), lax.rem(f, 4)
            tr = leaf_rows(t)
            fr = leaf_rows(f)
            k = affine(hi[tb, tr, :], lo[tb, tr, :], ncol[tb, tr, :],
                       uphi[fr, :], uplo[fr, :], upnrow[f, 0:1, :])
            weights = upw[q, yy]
            rhs = jnp.concatenate(
                [weights[zz].reshape(64, 128) * pick(tb, 3, yy * 4 + zz) for zz in range(4)], axis=0)
            acc[target, tr, :] += product_nn(k, rhs)
            return carry
        lax.fori_loop(0, 2 * count, body, 0)

    acc[...] = jnp.zeros_like(acc)

    wide_lane = lax.broadcasted_iota(jnp.int32, (ROWS, 64), 1)
    ones_col = jnp.where(wide_lane == 0, 1.0, 0.0)
    rt[0, 0] = jnp.transpose(jnp.concatenate([lab_ref[...], ones_col], axis=1))
    for slot in range(1, 6):
        rt[slot, 0, 64:128, :] = jnp.where(
            lax.broadcasted_iota(jnp.int32, (64, ROWS), 0) == 0, 1.0, 0.0)
        rt[slot, 1, 72:128, :] = jnp.zeros((56, ROWS), F32)

    first_leaf = gx * 16
    for t in range(2):
        row = jnp.zeros((1, 128), F32)
        for e in range(8):
            row += jnp.where(lane == near_ref[t, e] - first_leaf, 1.0, 0.0)
        masks[0, t:t + 1, :] = row
    row = jnp.zeros((1, 128), F32)
    for e in range(7):
        row += jnp.where(lane == flocal_ref[0, e], 1.0, 0.0)
    masks[0, 2:3, :] = row
    row = jnp.zeros((1, 128), F32)
    for e in range(15):
        row += jnp.where(lane == fupper_ref[0, e], 1.0, 0.0)
    masks[0, 3:4, :] = row
    masks[0, 4:8, :] = jnp.zeros((4, 128), F32)

    label_msgs = [send(rt.at[0, 0, 0:64], rt.at[slot, 0, 0:64], device)
                  for slot, device in ((1, sib), (2, chip(1, j)), (4, chip(3, j)))]
    mask_msgs = [send(masks.at[0], masks.at[slot], device)
                 for slot, device in ((1, sib), (2, chip(1, j)), (4, chip(3, j)))]

    skel_t = jnp.where(lax.broadcasted_iota(jnp.int32, (ROWS, SKEL), 0) == skel_ref[...], 1.0, 0.0)
    scol[...] = jnp.broadcast_to(jnp.max(skel_t, axis=1, keepdims=True), (ROWS, 128))
    skel = jnp.transpose(skel_t)
    srow[...] = jnp.broadcast_to(jnp.sum(skel, axis=0, keepdims=True), (8, ROWS))
    chosen_t = jnp.where(
        lax.broadcasted_iota(jnp.int32, (SKEL, SKEL), 0) + gy * SKEL == urow_ref[...], 1.0, 0.0)
    chosen = jnp.transpose(chosen_t).astype(BF16)
    select = dot_nn(chosen, skel.astype(BF16)).astype(BF16)

    own_copy.wait()
    for leaf in range(2):
        prep(0, leaf)

    rows_mine = dot_nn(select, hi[0]) + dot_nn(select, lo[0])
    for q in range(4):
        for h in range(2):
            contr[q, h] = rows_mine[64 * q + 32 * h:64 * q + 32 * h + 32, :]
    contr_msg = send(contr.at[:, other], contr_in, sib)

    def own_tile(i, carry):
        t, s = lax.div(i, 2), lax.rem(i, 2)
        kown[leaf_rows(t), leaf_rows(s)] = block_affine(0, t, 0, s)
        return carry
    lax.fori_loop(0, 4, own_tile, 0)
    inverse = 1.0 / jnp.sum(kown[...] * scol[:, 0:1], axis=0, keepdims=True)
    for t in range(2):
        tr = slice(t * 256, t * 256 + 256)
        total = jnp.zeros((256, 128), F32)
        for s in range(2):
            sr = slice(s * 256, s * 256 + 256)
            total += product_nt(kown[tr, sr] * inverse[:, sr], rt[0, 0, :, sr])
        rt[0, 1, :, tr] = jnp.transpose(total * scol[tr, :])
    weight_msgs = [send(rt.at[0, 1, 0:MSG], rt.at[slot, 1, 0:MSG], device)
                   for slot, device in ((1, sib), (2, chip(1, j)), (4, chip(3, j)))]

    def chip_sum(mine, incoming, total):
        for q in range(4):
            total[q] = mine[q, j] + incoming[q]

    def round_one(total, land):
        return [send(total.at[lax.rem(c + 3, 4)], land.at[0], chip(3, j)),
                send(total.at[lax.rem(c + 2, 4)], land.at[1], chip(1, j))]

    def round_two(total, land, middle, land_two):
        middle[0] = total[c] + land[0]
        middle[1] = total[after] + land[1]
        return [send(middle.at[0], land_two.at[1], chip(3, j)),
                send(middle.at[1], land_two.at[0], chip(1, j))]

    def finish(copies):
        for copy in copies:
            copy.wait_recv()

    contr_msg.wait_recv()
    chip_sum(contr, contr_in, part)
    ones = round_one(part, land1)
    send_bulk(1)

    def own_near(i, carry):
        t, s = lax.div(i, 2), lax.rem(i, 2)
        k = kown[leaf_rows(t), leaf_rows(s)]
        rows = lax.broadcasted_iota(jnp.int32, (256, 256), 0) + t * 256
        cols = lax.broadcasted_iota(jnp.int32, (256, 256), 1) + s * 256
        add_terms(jnp.where(rows == cols, 0.0, k), 0, t, 0, s, gy, 0)
        return carry
    lax.fori_loop(0, 4, own_near, 0)

    finish(ones)
    twos = round_two(part, land1, mid, land2)
    send_bulk(2)
    sib_points.wait_recv()
    label_msgs[0].wait_recv()
    mask_msgs[0].wait_recv()
    weight_msgs[0].wait_recv()
    for leaf in range(2):
        prep(1, leaf)

    finish(twos)
    quarter0 = mid[0] + land2[0]
    quarter1 = mid[1] + land2[1]
    uq[c, j] = quarter0
    uq[after, j] = quarter1
    up[0, y, z, j] = quarter0
    up[1, y, z, j] = quarter1
    threes = [send(uq.at[after, j], uq.at[after, j], chip(3, j)),
              send(uq.at[c, j], uq.at[c, j], chip(1, j))]

    def phase_one(buffer):
        return ([send(buffer.at[0, y, z, j], buffer.at[0, y, z, j], y_peer(s)) for s in (1, 2, 3)]
                + [send(buffer.at[1, y, z, j], buffer.at[1, y, z, j], z_peer(s)) for s in (1, 2, 3)])

    def phase_two(buffer):
        return ([send(buffer.at[0, :, z, j], buffer.at[0, :, z, j], z_peer(s)) for s in (1, 2, 3)]
                + [send(buffer.at[1, y, :, j], buffer.at[1, y, :, j], y_peer(s)) for s in (1, 2, 3)])

    up_one = phase_one(up)
    send_bulk(3)

    near(0, 1, 0, nodes[1], 0)
    near(0, 1, 1, nodes[1], 0)

    finish(threes)
    share = send(uq.at[:, j], uq.at[:, j], sib)
    send_bulk(4)
    finish(up_one)
    up_two = phase_two(up)
    share.wait_recv()

    def prep_upper(i, carry):
        value = uq[i].reshape(64, WIDTH)
        rows = pl.ds(pl.multiple_of(i * 64, 64), 64)
        high, low = split(value)
        uhi[rows, :] = high
        ulo[rows, :] = low
        norm = jnp.sum(value * value, axis=1, keepdims=True) * BETA
        uncol[rows, :] = jnp.broadcast_to(norm, (64, 128))
        return carry
    lax.fori_loop(0, 4, prep_upper, 0)
    partial_sum = jnp.zeros((SKEL, 128), F32)
    for s in range(2):
        sr = slice(s * 256, s * 256 + 256)
        k = affine(uhi[...], ulo[...], uncol[...], hi[0, sr, :], lo[0, sr, :], nrow[0, 0:1, sr])
        total = jnp.sum(k, axis=0, keepdims=True)
        taken = srow[0:1, sr] > 0.0
        shares = k * jnp.where(taken, 1.0 / total, 0.0)
        partial_sum += product_nt(shares, rt[0, 1, :, sr])
    for q in range(4):
        for h in range(2):
            wp[q, h] = partial_sum[64 * q + 32 * h:64 * q + 32 * h + 32, :]
    wp_msg = send(wp.at[:, other], wp_in, sib)
    send_bulk(5)

    for copy in label_msgs[1:] + mask_msgs[1:] + weight_msgs[1:]:
        copy.wait_recv()
    forward = []
    for slot in (2, 4):
        forward += [send(rt.at[slot, :, 0:MSG], rt.at[slot + 1, :, 0:MSG], sib),
                    send(masks.at[slot], masks.at[slot + 1], sib)]
    wp_msg.wait_recv()
    chip_sum(wp, wp_in, wpart)
    w_ones = round_one(wpart, wland1)
    send_bulk(6)

    def leaf_arrives(leaf):
        copies = []
        for step, slot in ((1, 2), (3, 4)):
            for at in range(leaf * CHUNKS // 2, (leaf + 1) * CHUNKS // 2):
                bulk[step, at].wait_recv()
            rows = slice(leaf * 256, leaf * 256 + 256)
            copies.append(send(pts.at[slot, rows], pts.at[slot + 1, rows], sib))
        return copies

    def prep_up(f, carry):
        q, yy = lax.div(f, 4), lax.rem(f, 4)
        for zz in range(4):
            value = up[q, yy, zz].reshape(64, WIDTH)
            rows = pl.ds(pl.multiple_of(f * 256 + zz * 64, 64), 64)
            high, low = split(value)
            uphi[rows, :] = high
            uplo[rows, :] = low
            norm = jnp.sum(value * value, axis=1, keepdims=True) * BETA
            uncol[zz * 64:zz * 64 + 64, :] = jnp.broadcast_to(norm, (64, 128))
        upnrow[f] = jnp.transpose(uncol[...])[0:8, :]
        return carry

    finish(w_ones)
    w_twos = round_two(wpart, wland1, wmid, wland2)
    send_bulk(7)
    first = leaf_arrives(0)
    for slot in (2, 4):
        prep(slot, 0)
        near(0, slot, 0, nodes[slot], 0)

    finish(w_twos)
    upw[0, y, z, j] = wmid[0] + wland2[0]
    upw[1, y, z, j] = wmid[1] + wland2[1]
    w_up_one = phase_one(upw)

    finish(up_two)
    up_share = send(up.at[:, :, :, j], up.at[:, :, :, j], sib)
    finish(forward)
    finish(first)
    for slot in (3, 5):
        prep(slot, 0)
        near(0, slot, 0, nodes[slot], 0)
    finish(w_up_one)
    w_up_two = phase_two(upw)
    up_share.wait_recv()
    lax.fori_loop(0, 8, prep_up, 0)
    finish(w_up_two)
    w_share = send(upw.at[:, :, :, j], upw.at[:, :, :, j], sib)
    w_share.wait_recv()
    far(0, 0, 0, 8)

    second = leaf_arrives(1)
    for slot in (2, 4):
        prep(slot, 1)
    finish(second)
    for slot in (3, 5):
        prep(slot, 1)

    for s in range(2):
        near(2, cross_slot, s, cross_node, 1)
    far(2, 1, 4, 4)
    ret_out[0] = jnp.transpose(acc[1])
    back_before = send(ret_out.at[0, 0:MSG], ret_in.at[0, 0:MSG], chip(3, j))
    for s in range(2):
        near(cross_slot, 2, s, nodes[2], 2)
    far(cross_slot, 2, 0, 4)
    ret_out[1] = jnp.transpose(acc[2])
    back_after = send(ret_out.at[1, 0:MSG], ret_in.at[1, 0:MSG], chip(1, crossed))

    for slot in (2, 4, 3, 5):
        near(0, slot, 1, nodes[slot], 0)
    back_before.wait_recv()
    back_after.wait_recv()
    returned = jnp.transpose(ret_in[0] + ret_in[1])
    out_ref[...] = acc[0] + returned

    for copy in started:
        copy.wait_send()


N_COPIES = 96


def on_device(points, labels, skeleton_rows, upper_rows, near_list, far_local, far_upper):
    vmem = pl.BlockSpec(memory_space=pltpu.VMEM)
    smem = pl.BlockSpec(memory_space=pltpu.SMEM)
    sums = pl.pallas_call(
        kernel,
        out_shape=jax.ShapeDtypeStruct((ROWS, 128), F32),
        in_specs=[pl.BlockSpec(memory_space=pl.ANY), vmem, vmem, vmem, smem, smem, smem],
        out_specs=vmem,
        scratch_shapes=[
            pltpu.VMEM((6, ROWS, WIDTH), F32),
            pltpu.VMEM((6, ROWS, WIDTH), BF16),
            pltpu.VMEM((6, ROWS, WIDTH), BF16),
            pltpu.VMEM((6, ROWS, 128), F32),
            pltpu.VMEM((6, 8, ROWS), F32),
            pltpu.VMEM((6, 2, 128, ROWS), F32),
            pltpu.VMEM((6, 8, 128), F32),
            pltpu.VMEM((ROWS, ROWS), F32),
            pltpu.VMEM((ROWS, 128), F32),
            pltpu.VMEM((8, ROWS), F32),
            pltpu.VMEM((4, 2, 32, WIDTH), F32),
            pltpu.VMEM((4, 32, WIDTH), F32),
            pltpu.VMEM((4, 32, WIDTH), F32),
            pltpu.VMEM((2, 32, WIDTH), F32),
            pltpu.VMEM((2, 32, WIDTH), F32),
            pltpu.VMEM((2, 32, WIDTH), F32),
            pltpu.VMEM((4, 2, 32, WIDTH), F32),
            pltpu.VMEM((SKEL, WIDTH), BF16),
            pltpu.VMEM((SKEL, WIDTH), BF16),
            pltpu.VMEM((SKEL, 128), F32),
            pltpu.VMEM((2, 4, 4, 2, 32, WIDTH), F32),
            pltpu.VMEM((2048, WIDTH), BF16),
            pltpu.VMEM((2048, WIDTH), BF16),
            pltpu.VMEM((8, 8, 256), F32),
            pltpu.VMEM((4, 2, 32, 128), F32),
            pltpu.VMEM((4, 32, 128), F32),
            pltpu.VMEM((4, 32, 128), F32),
            pltpu.VMEM((2, 32, 128), F32),
            pltpu.VMEM((2, 32, 128), F32),
            pltpu.VMEM((2, 32, 128), F32),
            pltpu.VMEM((2, 4, 4, 2, 32, 128), F32),
            pltpu.VMEM((3, ROWS, 128), F32),
            pltpu.VMEM((2, 128, ROWS), F32),
            pltpu.VMEM((2, 128, ROWS), F32),
            pltpu.SemaphoreType.DMA,
            pltpu.SemaphoreType.DMA((N_COPIES,)),
            pltpu.SemaphoreType.DMA((N_COPIES,)),
        ],
        compiler_params=pltpu.CompilerParams(
            collective_id=0, has_side_effects=True, vmem_limit_bytes=62 * 1024 * 1024),
        cost_estimate=pl.CostEstimate(
            flops=64 * 6 * 256 * 256 * 768, bytes_accessed=2 * 1024 * 1024, transcendentals=64 * 256 * 256),
    )(points, labels, skeleton_rows, upper_rows, near_list, far_local, far_upper)
    return sums[:, :LABELS] / sums[:, LABELS:LABELS + 1]


def solution(mesh):
    return jax.shard_map(
        on_device,
        mesh=mesh,
        in_specs=(
            P(("gx", "gy"), None),
            P(("gx", "gy"), None),
            P(("gx", "gy"), None),
            P("gx", None),
            P(("gx", "gy"), None),
            P(("gx", "gy"), None),
            P(("gx", "gy"), None),
        ),
        out_specs=P(("gx", "gy"), None),
        check_vma=False,
    )
```

time: 437 us -> 115 us (0.26)
  matrix products: 163 us -> 0 us
  waiting for transfers between devices: 111 us -> 0 us
  Pallas kernels: 0 us -> 110 us
  other arithmetic: 60.5 us -> 1.09 us
  blocking collectives: 43 us -> 0 us
  local copies, waits for them, and re-layouts: 29.2 us -> 3.69 us
  between operations: 13.4 us -> 0.02 us
  loops' own time: 12.8 us -> 0 us
    dot_general x89 -> x0, matrix products: 163 us -> none  [the longest x35 99 us: affinity(): jnp.einsum('id,jd->ij', left_rows, right_rows, precision=highest, preferr...]
    all_gather x5 -> x0, waiting for transfers between devices: 110 us -> none  [the longest x1 69.2 us: on_device(): sources = lax.all_gather(points, 'gy', axis=0, tiled=True)]
    pallas_call x0 -> x1, Pallas kernels: none -> 110 us  [on_device(): pl.pallas_call(kernel, out_shape=jax.ShapeDtypeStruct((ROWS, 128), F32),...]
    reduce_sum x36 -> x0, other arithmetic: 47.4 us -> none  [the longest x33 46 us: affinity(): right_sq = jnp.sum(right_rows * right_rows, axis=1)]
    all_gather x3 -> x0, blocking collectives: 43 us -> none  [the longest x1 18.7 us: on_device(): source_mass = lax.all_gather(whole_mass, 'gx', axis=0, tiled=True)]
    another operation x20 -> x0, loops' own time: 12.8 us -> none  [the longest x2 11.5 us: per_leaf(): result, _ = lax.scan(visit, zero_pair, listed)]
    eq x16 -> x0, other arithmetic: 11.1 us -> none  [add_tile(): owned = first_leaf + columns // LEAF == source_leaf]
    dynamic_slice x34 -> x0, local copies, waits for them, and re-layouts: 10.9 us -> none  [the longest x16 10.5 us: per_leaf(): result, _ = lax.scan(visit, zero_pair, listed)]
  transfers between devices with their start and end apart: 5 -> 0, of which waited for: 3 -> 0; matrix products, arithmetic and copies ran while one was open for 29% -> 0% of each run, Pallas kernels for 0% -> 0%
where the time goes in v1:
time: 115 us
  Pallas kernels  110 us (96%)
  local copies, waits for them, and re-layouts  3.69 us (3%)
    pallas_call x1, Pallas kernels, on_device(): pl.pallas_call(kernel, out_shape=jax.ShapeDtypeStruct((ROWS, 128), F32),...  110 us

profile of v1, /device:TPU:1, one launch (start us, length us, event | category | flops | bytes accessed | tf_op | source)
XLA Modules:
  0.0 114.6 jit_solution(7596819544929455497)
XLA Ops:
  0.0 1.7 %copy.12.lab_ref = f32[512,64]{1,0:T(8,128)} copy(f32[512,64]{0,1:T(8,128)} %param.8) | data formatting | bytes 262144 | tf_op args[1]
  1.7 109.8 %shard_map.73 = f32[512,128]{1,0:T(8,128)} custom-call(f32[512,768]{1,0:T(8,128)} %x_ref.1, f32[512,64]{1,0:T(8,128)} %copy.12.lab_ref, s32[1,256]{1,0:T(1,128)} %skel_ref.1, s32[1,256]{1,0:T(1,128)} %urow_ref.1, s32[2,8]{1,0:T(2,128)} %near_ref.1, s32[1,7]{1,0:T(1,128)} %flocal_ref.1, s32[1,15]{1,0:T(1,128)} %fupper_ref.1), custom_call_target="tpu_custom_call" | custom-call | flops 19327352832 | bytes 2097152 | tf_op jit(solution)/shard_map/pallas_call | solution.py:423
  111.5 1.2 %slice_reduce_fusion = f32[512]{0:T(512)S(1)} fusion(f32[512,128]{1,0:T(8,128)} %shard_map.73), kind=kLoop, calls=%fused_computation | loop fusion | bytes 4096 | tf_op jit(solution)/shard_map/slice | solution.py:472
  112.7 1.1 slice_divide_fusion
  113.8 0.8 copy.14

commit v2 on v1

v2 whole, which is shorter than its diff:
```python
import functools
import math

import jax
import jax.numpy as jnp
from jax import lax
from jax.experimental import pallas as pl
from jax.experimental.pallas import tpu as pltpu
from jax.sharding import PartitionSpec as P

MESH = pl.DeviceIdType.MESH
F32, BF16 = jnp.float32, jnp.bfloat16
ROWS, WIDTH, LABELS, SKEL, LEAF = 512, 768, 64, 256, 256
MSG = 72
CHUNKS = (32, 32, 32, 32, 64, 64, 128, 128)
BETA = 25.0 * math.log2(math.e)


def dot_nt(a, b):
    return lax.dot_general(a, b, (((1,), (1,)), ((), ())), preferred_element_type=F32)


def dot_nn(a, b):
    return jnp.dot(a, b, preferred_element_type=F32)


def split(value):
    high = value.astype(BF16)
    return high, (value - high.astype(F32)).astype(BF16)


def kernel(x_ref, lab_ref, skel_ref, urow_ref, near_ref, flocal_ref, fupper_ref, out_ref,
           pts, hi, lo, ncol, nrow, rt, masks, kown, scol, srow,
           contr, contr_in, part, land1, mid, land2, uq, uhi, ulo, uncol,
           up, uphi, uplo, upnrow,
           wp, wp_in, wpart, wland1, wmid, wland2, upw, kf_hi, kf_lo, kn_hi, kn_lo,
           acc, ret_out, ret_in,
           own_sem, s_sem, r_sem):
    gx, gy = lax.axis_index("gx"), lax.axis_index("gy")
    c, j = lax.div(gy, 2), lax.rem(gy, 2)
    y, z = lax.div(gx, 4), lax.rem(gx, 4)
    half = lax.div(c, 2)
    other = 1 - j
    crossed = lax.rem(j + half, 2)
    before, after = lax.rem(c + 3, 4), lax.rem(c + 1, 4)

    def chip(step, core):
        return (gx, lax.rem(c + step, 4) * 2 + core)

    sib = (gx, c * 2 + other)

    def y_peer(step):
        return (lax.rem(y + step, 4) * 4 + z, gy)

    def z_peer(step):
        return (y * 4 + lax.rem(z + step, 4), gy)

    own_copies = [pltpu.make_async_copy(x_ref.at[pl.ds(256 * leaf, 256)], pts.at[leaf], own_sem.at[leaf])
                  for leaf in range(2)]
    own_copies.append(pltpu.make_async_copy(lab_ref, rt.at[0, 0, 0:64], own_sem.at[2]))
    for copy in own_copies:
        copy.start()

    partners = [sib] + [chip(s, k) for s in (1, 3) for k in (j, other)]
    partners += [y_peer(s) for s in (1, 2, 3)] + [z_peer(s) for s in (1, 2, 3)]
    barrier = pltpu.get_barrier_semaphore()
    for partner in partners:
        pl.semaphore_signal(barrier, inc=1, device_id=partner, device_id_type=MESH)
    pl.semaphore_wait(barrier, len(partners))

    started = []

    def send(src, dst, device):
        at = len(started)
        copy = pltpu.make_async_remote_copy(
            src_ref=src, dst_ref=dst, send_sem=s_sem.at[at], recv_sem=r_sem.at[at],
            device_id=device, device_id_type=MESH)
        copy.start()
        started.append(copy)
        return copy

    def finish(copies):
        for copy in copies:
            copy.wait_recv()

    nodes = [gy, c * 2 + other, before * 2 + j, before * 2 + other, after * 2 + j, after * 2 + other]
    cross_slot, cross_node, cross_leaf = 4 + half, after * 2 + crossed, 5 + 4 * half

    bulk = {1: [], 3: []}

    def send_bulk(count=1):
        for _ in range(count):
            at = len(bulk[1])
            first, size = sum(CHUNKS[:at]), CHUNKS[at]
            leaf, rows = first // 256, pl.ds(first % 256, size)
            src = x_ref.at[pl.ds(first, size)]
            bulk[1].append(send(src, pts.at[4 + 2 * leaf, rows], chip(1, j)))
            bulk[3].append(send(src, pts.at[5 + 2 * leaf, rows], chip(3, j)))

    label_msgs = [send(lab_ref, rt.at[slot, 0, 0:64], device)
                  for slot, device in ((2, chip(1, j)), (4, chip(3, j)), (1, sib))]
    send_bulk()
    sib_points = [send(x_ref.at[pl.ds(256 * leaf, 256)], pts.at[2 + leaf], sib) for leaf in range(2)]

    skel_t = jnp.where(lax.broadcasted_iota(jnp.int32, (ROWS, SKEL), 0) == skel_ref[...], 1.0, 0.0)
    scol[...] = jnp.broadcast_to(jnp.max(skel_t, axis=1, keepdims=True), (ROWS, 128))
    skel = jnp.transpose(skel_t)
    srow[...] = jnp.broadcast_to(jnp.sum(skel, axis=0, keepdims=True), (8, ROWS))
    chosen_t = jnp.where(
        lax.broadcasted_iota(jnp.int32, (SKEL, SKEL), 0) + gy * SKEL == urow_ref[...], 1.0, 0.0)
    chosen = jnp.transpose(chosen_t).astype(BF16)
    select = dot_nn(chosen, skel.astype(BF16)).astype(BF16)

    def prep(leaf, first, size):
        def body(i, carry):
            rows = pl.ds(pl.multiple_of(first + i * 128, 128), 128)
            value = pts[leaf, rows, :]
            high, low = split(value)
            hi[leaf, rows, :] = high
            lo[leaf, rows, :] = low
            norm = jnp.sum(value * value, axis=1, keepdims=True) * BETA
            wide = jnp.broadcast_to(norm, (128, 128))
            ncol[leaf, rows, :] = wide
            nrow[leaf, :, rows] = jnp.transpose(wide)[0:8, :]
            return carry
        lax.fori_loop(0, size // 128, body, 0)

    def many(parts, axis):
        return parts[0] if len(parts) == 1 else jnp.concatenate(parts, axis=axis)

    def affine(targets, sources):
        t_hi, t_lo, t_col = targets
        s_hi, s_lo, s_row = sources
        cross = dot_nt(t_hi, s_hi) + dot_nt(t_hi, s_lo) + dot_nt(t_lo, s_hi)
        wide = jnp.concatenate([t_col] * (s_hi.shape[0] // 128), axis=1)
        return jnp.exp2(cross * (2.0 * BETA) - wide - s_row)

    def as_targets(pieces):
        return (many([hi[l, f:f + n, :] for l, f, n in pieces], 0),
                many([lo[l, f:f + n, :] for l, f, n in pieces], 0),
                many([ncol[l, f:f + n, :] for l, f, n in pieces], 0))

    def as_sources(pieces):
        return (many([hi[l, f:f + n, :] for l, f, n in pieces], 0),
                many([lo[l, f:f + n, :] for l, f, n in pieces], 0),
                many([nrow[l, 0:1, f:f + n] for l, f, n in pieces], 1))

    def product_nt(k, rhs):
        k_hi, k_lo = split(k)
        r_hi, r_lo = split(rhs)
        both = dot_nt(k_hi, jnp.concatenate([r_hi, r_lo], axis=0))
        return both[:, :128] + both[:, 128:] + dot_nt(k_lo, r_hi)

    def product_nn(k_hi, k_lo, rhs):
        r_hi, r_lo = split(rhs)
        both = dot_nn(k_hi, jnp.concatenate([r_hi, r_lo], axis=1))
        return both[:, :128] + both[:, 128:] + dot_nn(k_lo, r_hi)

    lane = lax.broadcasted_iota(jnp.int32, (1, 128), 1)

    def pick(slot, row, at):
        return jnp.sum(jnp.where(lane == at, masks[slot, row:row + 1, :], 0.0), axis=1, keepdims=True)

    def near_rhs(slot, t, sources):
        return many([pick(slot, t, 2 * node + s) * rt[sl, 0, :, 256 * s + f:256 * s + f + n]
                     + pick(slot, 2, node) * rt[sl, 1, :, 256 * s + f:256 * s + f + n]
                     for sl, node, s, f, n in sources], 1)

    def near(target, slot, targets, source_pieces, source_terms):
        k = affine(as_targets([(l, f, n) for l, _, f, n in targets]), as_sources(source_pieces))
        at = 0
        for _, t, f, n in targets:
            acc[target, 256 * t + f:256 * t + f + n, :] += product_nt(
                k[at:at + n], near_rhs(slot, t, source_terms))
            at += n

    OWN = [(0, 0, 0, 256), (1, 1, 0, 256)]

    def up_sources(q, m):
        rows = pl.ds(pl.multiple_of((q * 4 + m) * 256, 256), 256)
        return uphi[rows, :], uplo[rows, :], upnrow[q * 4 + m, 0:1, :]

    def up_pair(parts):
        loaded = [up_sources(q, m) for q, m in parts]
        return (many([p[0] for p in loaded], 0), many([p[1] for p in loaded], 0), many([p[2] for p in loaded], 1))

    def up_rhs(slot, q, m):
        weights = upw[q, m]
        parts = []
        for n in range(4):
            cluster = n * 4 + m if q == 0 else m * 4 + n
            parts.append(weights[n].reshape(64, 128) * pick(slot, 3, cluster))
        return jnp.concatenate(parts, axis=0)

    acc[...] = jnp.zeros_like(acc)

    for slot in range(6):
        rt[slot, 0, 64:128, :] = jnp.where(
            lax.broadcasted_iota(jnp.int32, (64, ROWS), 0) == 0, 1.0, 0.0)
        rt[slot, 1, 72:128, :] = jnp.zeros((56, ROWS), F32)

    own_copies[0].wait()
    own_copies[1].wait()
    for leaf in range(2):
        prep(leaf, 0, 256)

    rows_mine = jnp.zeros((SKEL, WIDTH), F32)
    for leaf in range(2):
        chosen_rows = select[:, 256 * leaf:256 * leaf + 256]
        rows_mine += dot_nn(chosen_rows, hi[leaf]) + dot_nn(chosen_rows, lo[leaf])
    for q in range(4):
        for h in range(2):
            contr[q, h] = rows_mine[64 * q + 32 * h:64 * q + 32 * h + 32, :]
    contr_msg = send(contr.at[:, other], contr_in, sib)

    def mask_row(entries):
        row = jnp.zeros((1, 128), F32)
        for entry in entries:
            row += jnp.where(lane == entry, 1.0, 0.0)
        return row

    for t in range(2):
        masks[0, t:t + 1, :] = mask_row([near_ref[t, e] - gx * 16 for e in range(8)])
    masks[0, 2:3, :] = mask_row([flocal_ref[0, e] for e in range(7)])
    masks[0, 3:4, :] = mask_row([fupper_ref[0, e] for e in range(15)])
    masks[0, 4:8, :] = jnp.zeros((4, 128), F32)
    mask_msgs = [send(masks.at[0], masks.at[slot], device)
                 for slot, device in ((1, sib), (2, chip(1, j)), (4, chip(3, j)))]

    def chip_sum(mine, incoming, total):
        for q in range(4):
            total[q] = mine[q, j] + incoming[q]

    def round_one(total, land):
        return [send(total.at[lax.rem(c + 3, 4)], land.at[0], chip(3, j)),
                send(total.at[lax.rem(c + 2, 4)], land.at[1], chip(1, j))]

    def round_two(total, land, middle, land_two):
        middle[0] = total[c] + land[0]
        middle[1] = total[after] + land[1]
        return [send(middle.at[0], land_two.at[1], chip(3, j)),
                send(middle.at[1], land_two.at[0], chip(1, j))]

    contr_msg.wait_recv()
    chip_sum(contr, contr_in, part)
    ones = round_one(part, land1)
    send_bulk()

    kown[...] = affine(as_targets([(0, 0, 256), (1, 0, 256)]), as_sources([(0, 0, 256), (1, 0, 256)]))
    own_copies[2].wait()
    inverse = 1.0 / jnp.sum(kown[...] * scol[:, 0:1], axis=0, keepdims=True)
    lower = product_nt(kown[...] * inverse, rt[0, 0]) * scol[...]

    finish(ones)
    twos = round_two(part, land1, mid, land2)
    send_bulk()

    rt[0, 1] = jnp.transpose(lower)

    rows_at = lax.broadcasted_iota(jnp.int32, (256, ROWS), 0)
    cols_at = lax.broadcasted_iota(jnp.int32, (256, ROWS), 1)
    for t in range(2):
        k = jnp.where(rows_at + 256 * t == cols_at, 0.0, kown[256 * t:256 * t + 256, :])
        acc[0, 256 * t:256 * t + 256, :] += product_nt(
            k, near_rhs(0, t, [(0, gy, 0, 0, 256), (0, gy, 1, 0, 256)]))

    finish(twos)
    quarter0 = mid[0] + land2[0]
    quarter1 = mid[1] + land2[1]
    uq[c, j] = quarter0
    uq[after, j] = quarter1
    up[0, z, y, j] = quarter0
    up[1, y, z, j] = quarter1
    threes = [send(uq.at[after, j], uq.at[after, j], chip(3, j)),
              send(uq.at[c, j], uq.at[c, j], chip(1, j))]

    def phase_one(buffer):
        return ([send(buffer.at[0, z, y, j], buffer.at[0, z, y, j], y_peer(s)) for s in (1, 3, 2)]
                + [send(buffer.at[1, y, z, j], buffer.at[1, y, z, j], z_peer(s)) for s in (1, 3, 2)])

    def phase_two(buffer):
        return {s: [send(buffer.at[0, z, :, j], buffer.at[0, z, :, j], z_peer(s)),
                    send(buffer.at[1, y, :, j], buffer.at[1, y, :, j], y_peer(s))] for s in (1, 3, 2)}

    def majors(step):
        return lax.rem(z + 4 - step, 4), lax.rem(y + 4 - step, 4)

    def share_step(buffer, step):
        m0, m1 = majors(step)
        return [send(buffer.at[0, m0, :, j], buffer.at[0, m0, :, j], sib),
                send(buffer.at[1, m1, :, j], buffer.at[1, m1, :, j], sib)]

    up_one = phase_one(up)
    send_bulk()
    weight_msgs = [send(rt.at[0, 1, 0:MSG], rt.at[slot, 1, 0:MSG], device)
                   for slot, device in ((1, sib), (2, chip(1, j)), (4, chip(3, j)))]

    finish(sib_points)
    label_msgs[2].wait_recv()
    mask_msgs[0].wait_recv()
    for leaf in range(2):
        prep(2 + leaf, 0, 256)

    finish(up_one)
    up_two = phase_two(up)
    up_share = {0: share_step(up, 0)}

    finish(threes)
    share = send(uq.at[:, j], uq.at[:, j], sib)
    weight_msgs[0].wait_recv()
    near(0, 0, OWN, [(2, 0, 256), (3, 0, 256)], [(1, nodes[1], 0, 0, 256), (1, nodes[1], 1, 0, 256)])
    send_bulk()
    share.wait_recv()

    def prep_upper(i, carry):
        value = uq[i].reshape(64, WIDTH)
        rows = pl.ds(pl.multiple_of(i * 64, 64), 64)
        high, low = split(value)
        uhi[rows, :] = high
        ulo[rows, :] = low
        norm = jnp.sum(value * value, axis=1, keepdims=True) * BETA
        uncol[rows, :] = jnp.broadcast_to(norm, (64, 128))
        return carry
    lax.fori_loop(0, 4, prep_upper, 0)
    k = affine((uhi[...], ulo[...], uncol[...]), as_sources([(0, 0, 256), (1, 0, 256)]))
    total = jnp.sum(k, axis=0, keepdims=True)
    shares = k * jnp.where(srow[0:1, :] > 0.0, 1.0 / total, 0.0)
    partial_sum = product_nt(shares, rt[0, 1])
    for q in range(4):
        for h in range(2):
            wp[q, h] = partial_sum[64 * q + 32 * h:64 * q + 32 * h + 32, :]
    wp_msg = send(wp.at[:, other], wp_in, sib)

    def prep_up(q, m):
        def body(n, carry):
            value = up[q, m, n].reshape(64, WIDTH)
            rows = pl.ds(pl.multiple_of((q * 4 + m) * 256 + n * 64, 64), 64)
            high, low = split(value)
            uphi[rows, :] = high
            uplo[rows, :] = low
            norm = jnp.sum(value * value, axis=1, keepdims=True) * BETA
            uncol[pl.ds(pl.multiple_of(n * 64, 64), 64), :] = jnp.broadcast_to(norm, (64, 128))
            return carry
        lax.fori_loop(0, 4, body, 0)
        upnrow[q * 4 + m] = jnp.transpose(uncol[...])[0:8, :]

    def far_own(step):
        m0, m1 = majors(step)
        prep_up(0, m0)
        prep_up(1, m1)
        k_hi, k_lo = split(affine(as_targets([(0, 0, 256), (1, 0, 256)]), up_pair([(0, m0), (1, m1)])))
        kf_hi[step] = k_hi
        kf_lo[step] = k_lo

    finish(up_share[0])
    far_own(0)

    wp_msg.wait_recv()
    chip_sum(wp, wp_in, wpart)
    w_ones = round_one(wpart, wland1)
    send_bulk()

    finish(label_msgs[:2] + mask_msgs[1:] + weight_msgs[1:])
    forward = []
    for slot in (2, 4):
        forward += [send(rt.at[slot, :, 0:MSG], rt.at[slot + 1, :, 0:MSG], sib),
                    send(masks.at[slot], masks.at[slot + 1], sib)]
    finish(w_ones)
    w_twos = round_two(wpart, wland1, wmid, wland2)
    send_bulk(len(CHUNKS) - len(bulk[1]))

    finish(up_two[1])
    up_share[1] = share_step(up, 1)
    finish(up_two[3])
    up_share[3] = share_step(up, 3)

    finish(w_twos)
    upw[0, z, y, j] = wmid[0] + wland2[0]
    upw[1, y, z, j] = wmid[1] + wland2[1]
    w_up_one = phase_one(upw)

    finish(up_share[1])
    far_own(1)
    finish(up_share[3])
    far_own(3)

    taken = [0]

    def piece_arrives(leaf, first, size):
        end = 256 * leaf + first + size
        while taken[0] < len(CHUNKS) and sum(CHUNKS[:taken[0] + 1]) <= end:
            bulk[1][taken[0]].wait_recv()
            bulk[3][taken[0]].wait_recv()
            taken[0] += 1
        rows = pl.ds(first, size)
        return [send(pts.at[4 + 2 * leaf + side, rows], pts.at[8 + 2 * leaf + side, rows], sib)
                for side in range(2)]

    passed = piece_arrives(0, 0, 256)
    for buffer in (4, 5):
        prep(buffer, 0, 256)
    near(0, 0, OWN, [(4, 0, 256), (5, 0, 256)], [(2, nodes[2], 0, 0, 256), (4, nodes[4], 0, 0, 256)])
    finish(passed)
    finish(forward)
    for buffer in (8, 9):
        prep(buffer, 0, 256)
    near(0, 0, OWN, [(8, 0, 256), (9, 0, 256)], [(3, nodes[3], 0, 0, 256), (5, nodes[5], 0, 0, 256)])

    finish(up_two[2])
    up_share[2] = share_step(up, 2)
    finish(w_up_one)
    w_up_two = phase_two(upw)
    finish(up_share[2])
    far_own(2)

    def far_kernel(target_pieces, q, m):
        return split(affine(as_targets(target_pieces), up_pair([(q, m), (q, m + 1)])))

    for side, (leaf, q) in enumerate(((4, 1), (cross_leaf, 0))):
        for m in (0, 2):
            k_hi, k_lo = far_kernel([(leaf, 0, 256)], q, m)
            kn_hi[side, m // 2] = k_hi
            kn_lo[side, m // 2] = k_lo

    for s in (1, 3, 2):
        finish(w_up_two[s])
    w_share = [send(upw.at[:, :, :, j], upw.at[:, :, :, j], sib)]
    finish(w_share)

    for step in range(4):
        m0, m1 = majors(step)
        rhs = jnp.concatenate([up_rhs(0, 0, m0), up_rhs(0, 1, m1)], axis=0)
        acc[0] += product_nn(kf_hi[step], kf_lo[step], rhs)

    def far_terms(slot, q, m):
        return jnp.concatenate([up_rhs(slot, q, m), up_rhs(slot, q, m + 1)], axis=0)

    for side, (slot, q) in enumerate(((2, 1), (cross_slot, 0))):
        for m in (0, 2):
            acc[1 + side, 0:256, :] += product_nn(kn_hi[side, m // 2], kn_lo[side, m // 2], far_terms(slot, q, m))

    for first in (0, 128):
        passed = piece_arrives(1, first, 128)
        for buffer in (6, 7):
            prep(buffer, first, 128)
        finish(passed)
        for buffer in (10, 11):
            prep(buffer, first, 128)

        def own_piece():
            near(0, 0, OWN, [(b, first, 128) for b in (6, 7, 10, 11)],
                 [(sl, nodes[sl], 1, first, 128) for sl in (2, 4, 3, 5)])

        if first == 0:
            own_piece()
        for side, (slot, leaf, q) in enumerate(((2, 6, 1), (cross_slot, cross_leaf + 2, 0))):
            for m in (0, 2):
                k_hi, k_lo = far_kernel([(leaf, first, 128)], q, m)
                acc[1 + side, 256 + first:384 + first, :] += product_nn(k_hi, k_lo, far_terms(slot, q, m))

    sides = ((2, nodes[2], 4), (cross_slot, cross_node, cross_leaf))
    backs = []
    for side in range(2):
        slot, _, leaf = sides[side]
        from_slot, from_node, from_leaf = sides[1 - side]
        near(1 + side, slot, [(leaf, 0, 0, 256), (leaf + 2, 1, 0, 256)],
             [(from_leaf, 0, 256), (from_leaf + 2, 0, 256)],
             [(from_slot, from_node, 0, 0, 256), (from_slot, from_node, 1, 0, 256)])
        ret_out[side] = jnp.transpose(acc[1 + side])
        backs.append(send(ret_out.at[side, 0:MSG], ret_in.at[side, 0:MSG],
                          chip(3, j) if side == 0 else chip(1, crossed)))
    own_piece()
    finish(backs)
    sums = jnp.transpose(acc[0])[0:MSG] + ret_in[0, 0:MSG] + ret_in[1, 0:MSG]
    out_ref[...] = sums[0:LABELS] / sums[LABELS:LABELS + 1]

    for copy in started:
        copy.wait_send()


N_COPIES = 110


def on_device(points, labels, skeleton_rows, upper_rows, near_list, far_local, far_upper):
    vmem = pl.BlockSpec(memory_space=pltpu.VMEM)
    smem = pl.BlockSpec(memory_space=pltpu.SMEM)
    hbm = pl.BlockSpec(memory_space=pl.ANY)
    result = pl.pallas_call(
        kernel,
        out_shape=jax.ShapeDtypeStruct((LABELS, ROWS), F32),
        in_specs=[hbm, hbm, vmem, vmem, smem, smem, smem],
        out_specs=vmem,
        scratch_shapes=[
            pltpu.VMEM((12, LEAF, WIDTH), F32),
            pltpu.VMEM((12, LEAF, WIDTH), BF16),
            pltpu.VMEM((12, LEAF, WIDTH), BF16),
            pltpu.VMEM((12, LEAF, 128), F32),
            pltpu.VMEM((12, 8, LEAF), F32),
            pltpu.VMEM((6, 2, 128, ROWS), F32),
            pltpu.VMEM((6, 8, 128), F32),
            pltpu.VMEM((ROWS, ROWS), F32),
            pltpu.VMEM((ROWS, 128), F32),
            pltpu.VMEM((8, ROWS), F32),
            pltpu.VMEM((4, 2, 32, WIDTH), F32),
            pltpu.VMEM((4, 32, WIDTH), F32),
            pltpu.VMEM((4, 32, WIDTH), F32),
            pltpu.VMEM((2, 32, WIDTH), F32),
            pltpu.VMEM((2, 32, WIDTH), F32),
            pltpu.VMEM((2, 32, WIDTH), F32),
            pltpu.VMEM((4, 2, 32, WIDTH), F32),
            pltpu.VMEM((SKEL, WIDTH), BF16),
            pltpu.VMEM((SKEL, WIDTH), BF16),
            pltpu.VMEM((SKEL, 128), F32),
            pltpu.VMEM((2, 4, 4, 2, 32, WIDTH), F32),
            pltpu.VMEM((2048, WIDTH), BF16),
            pltpu.VMEM((2048, WIDTH), BF16),
            pltpu.VMEM((8, 8, 256), F32),
            pltpu.VMEM((4, 2, 32, 128), F32),
            pltpu.VMEM((4, 32, 128), F32),
            pltpu.VMEM((4, 32, 128), F32),
            pltpu.VMEM((2, 32, 128), F32),
            pltpu.VMEM((2, 32, 128), F32),
            pltpu.VMEM((2, 32, 128), F32),
            pltpu.VMEM((2, 4, 4, 2, 32, 128), F32),
            pltpu.VMEM((4, ROWS, ROWS), BF16),
            pltpu.VMEM((4, ROWS, ROWS), BF16),
            pltpu.VMEM((2, 2, LEAF, ROWS), BF16),
            pltpu.VMEM((2, 2, LEAF, ROWS), BF16),
            pltpu.VMEM((3, ROWS, 128), F32),
            pltpu.VMEM((2, 128, ROWS), F32),
            pltpu.VMEM((2, 128, ROWS), F32),
            pltpu.SemaphoreType.DMA((3,)),
            pltpu.SemaphoreType.DMA((N_COPIES,)),
            pltpu.SemaphoreType.DMA((N_COPIES,)),
        ],
        compiler_params=pltpu.CompilerParams(
            collective_id=0, has_side_effects=True, vmem_limit_bytes=62 * 1024 * 1024),
        cost_estimate=pl.CostEstimate(
            flops=64 * 6 * 256 * 256 * 768, bytes_accessed=2 * 1024 * 1024, transcendentals=64 * 256 * 256),
    )(points, labels.T, skeleton_rows, upper_rows, near_list, far_local, far_upper)
    return result.T


def solution(mesh):
    return jax.shard_map(
        on_device,
        mesh=mesh,
        in_specs=(
            P(("gx", "gy"), None),
            P(("gx", "gy"), None),
            P(("gx", "gy"), None),
            P("gx", None),
            P(("gx", "gy"), None),
            P(("gx", "gy"), None),
            P(("gx", "gy"), None),
        ),
        out_specs=P(("gx", "gy"), None),
        check_vma=False,
    )
```

time: 115 us -> 96.3 us (0.84)
  Pallas kernels: 110 us -> 94.6 us
  local copies, waits for them, and re-layouts: 3.69 us -> 1.57 us
    pallas_call x1, Pallas kernels: 110 us -> 94.6 us  [on_device(): pl.pallas_call(kernel, out_shape=jax.ShapeDtypeStruct((LABELS, ROWS), F32...]
    slice x1 -> x0, local copies, waits for them, and re-layouts: 1.18 us -> none  [on_device(): return sums[:, :LABELS] / sums[:, LABELS:LABELS + 1]]
where the time goes in v2:
time: 96.3 us; the launch traced here: 96.2 us
  Pallas kernels  94.6 us (98%)
  local copies, waits for them, and re-layouts  1.57 us (2%)
    pallas_call x1, Pallas kernels, on_device(): pl.pallas_call(kernel, out_shape=jax.ShapeDtypeStruct((LABELS, ROWS), F32...  94.6 us

profile of v2, /device:TPU:1, one launch (start us, length us, event | category | flops | bytes accessed | tf_op | source)
XLA Modules:
  0.0 96.2 jit_solution(2756742149836520455)
XLA Ops:
  0.0 94.6 %shard_map.73 = f32[64,512]{1,0:T(8,128)} custom-call(f32[512,768]{1,0:T(8,128)} %x_ref.1, f32[64,512]{1,0:T(8,128)} %bitcast.3, s32[1,256]{1,0:T(1,128)} %skel_ref.1, s32[1,256]{1,0:T(1,128)} %urow_ref.1, s32[2,8]{1,0:T(2,128)} %near_ref.1, s32[1,7]{1,0:T(1,128)} %flocal_ref.1, s32[1,15]{1,0:T(1,128)} %fupper_ref.1), custom_call_target="tpu_custom_call" | custom-call | flops 19327352832 | bytes 2097152 | tf_op jit(solution)/shard_map/pallas_call | solution.py:488
  94.6 1.6 %copy.9 = f32[512,64]{0,1:T(8,128)} copy(f32[512,64]{0,1:T(8,128)} %bitcast.2) | data formatting | bytes 262144

commit v3 on v2

--- a/solution.py
+++ b/solution.py
@@ -31,7 +31,7 @@
 
 def kernel(x_ref, lab_ref, skel_ref, urow_ref, near_ref, flocal_ref, fupper_ref, out_ref,
            pts, hi, lo, ncol, nrow, rt, masks, kown, scol, srow,
-           contr, contr_in, part, land1, mid, land2, uq, uhi, ulo, uncol,
+           contr, contr_in, part, land1, mid, land2, uq,
            up, uphi, uplo, upnrow,
            wp, wp_in, wpart, wland1, wmid, wland2, upw, kf_hi, kf_lo, kn_hi, kn_lo,
            acc, ret_out, ret_in,
@@ -66,6 +66,37 @@
     barrier = pltpu.get_barrier_semaphore()
     for partner in partners:
         pl.semaphore_signal(barrier, inc=1, device_id=partner, device_id_type=MESH)
+
+    skel_t = jnp.where(lax.broadcasted_iota(jnp.int32, (ROWS, SKEL), 0) == skel_ref[...], 1.0, 0.0)
+    scol[...] = jnp.broadcast_to(jnp.max(skel_t, axis=1, keepdims=True), (ROWS, 128))
+    skel = jnp.transpose(skel_t)
+    srow[...] = jnp.broadcast_to(jnp.sum(skel, axis=0, keepdims=True), (8, ROWS))
+    chosen_t = jnp.where(
+        lax.broadcasted_iota(jnp.int32, (SKEL, SKEL), 0) + gy * SKEL == urow_ref[...], 1.0, 0.0)
+    chosen = jnp.transpose(chosen_t).astype(BF16)
+    select = dot_nn(chosen, skel.astype(BF16)).astype(BF16)
+
+    def prep(leaf):
+        value = pts[leaf]
+        high, low = split(value)
+        hi[leaf] = high
+        lo[leaf] = low
+        wide = jnp.broadcast_to(jnp.sum(value * value, axis=1, keepdims=True) * BETA, (256, 128))
+        ncol[leaf] = wide
+        nrow[leaf] = jnp.transpose(wide)[0:8, :]
+
+    for leaf in range(2):
+        own_copies[leaf].wait()
+        prep(leaf)
+
+    rows_mine = jnp.zeros((SKEL, WIDTH), F32)
+    for leaf in range(2):
+        chosen_rows = select[:, 256 * leaf:256 * leaf + 256]
+        rows_mine += dot_nn(chosen_rows, hi[leaf]) + dot_nn(chosen_rows, lo[leaf])
+    for q in range(4):
+        for h in range(2):
+            contr[q, h] = rows_mine[64 * q + 32 * h:64 * q + 32 * h + 32, :]
+
     pl.semaphore_wait(barrier, len(partners))
 
     started = []
@@ -83,8 +114,8 @@
         for copy in copies:
             copy.wait_recv()
 
-    nodes = [gy, c * 2 + other, before * 2 + j, before * 2 + other, after * 2 + j, after * 2 + other]
-    cross_slot, cross_node, cross_leaf = 4 + half, after * 2 + crossed, 5 + 4 * half
+    nodes = [gy, c * 2 + other, before * 2 + j, after * 2 + crossed]
+    to_after, to_before = chip(1, j), chip(3, lax.rem(j + lax.div(before, 2), 2))
 
     bulk = {1: [], 3: []}
 
@@ -94,36 +125,14 @@
             first, size = sum(CHUNKS[:at]), CHUNKS[at]
             leaf, rows = first // 256, pl.ds(first % 256, size)
             src = x_ref.at[pl.ds(first, size)]
-            bulk[1].append(send(src, pts.at[4 + 2 * leaf, rows], chip(1, j)))
-            bulk[3].append(send(src, pts.at[5 + 2 * leaf, rows], chip(3, j)))
-
+            bulk[1].append(send(src, pts.at[4 + 2 * leaf, rows], to_after))
+            bulk[3].append(send(src, pts.at[5 + 2 * leaf, rows], to_before))
+
+    contr_msg = send(contr.at[:, other], contr_in, sib)
     label_msgs = [send(lab_ref, rt.at[slot, 0, 0:64], device)
-                  for slot, device in ((2, chip(1, j)), (4, chip(3, j)), (1, sib))]
+                  for slot, device in ((2, to_after), (3, to_before), (1, sib))]
     send_bulk()
     sib_points = [send(x_ref.at[pl.ds(256 * leaf, 256)], pts.at[2 + leaf], sib) for leaf in range(2)]
-
-    skel_t = jnp.where(lax.broadcasted_iota(jnp.int32, (ROWS, SKEL), 0) == skel_ref[...], 1.0, 0.0)
-    scol[...] = jnp.broadcast_to(jnp.max(skel_t, axis=1, keepdims=True), (ROWS, 128))
-    skel = jnp.transpose(skel_t)
-    srow[...] = jnp.broadcast_to(jnp.sum(skel, axis=0, keepdims=True), (8, ROWS))
-    chosen_t = jnp.where(
-        lax.broadcasted_iota(jnp.int32, (SKEL, SKEL), 0) + gy * SKEL == urow_ref[...], 1.0, 0.0)
-    chosen = jnp.transpose(chosen_t).astype(BF16)
-    select = dot_nn(chosen, skel.astype(BF16)).astype(BF16)
-
-    def prep(leaf, first, size):
-        def body(i, carry):
-            rows = pl.ds(pl.multiple_of(first + i * 128, 128), 128)
-            value = pts[leaf, rows, :]
-            high, low = split(value)
-            hi[leaf, rows, :] = high
-            lo[leaf, rows, :] = low
-            norm = jnp.sum(value * value, axis=1, keepdims=True) * BETA
-            wide = jnp.broadcast_to(norm, (128, 128))
-            ncol[leaf, rows, :] = wide
-            nrow[leaf, :, rows] = jnp.transpose(wide)[0:8, :]
-            return carry
-        lax.fori_loop(0, size // 128, body, 0)
 
     def many(parts, axis):
         return parts[0] if len(parts) == 1 else jnp.concatenate(parts, axis=axis)
@@ -194,24 +203,11 @@
 
     acc[...] = jnp.zeros_like(acc)
 
-    for slot in range(6):
+    for slot in range(4):
         rt[slot, 0, 64:128, :] = jnp.where(
             lax.broadcasted_iota(jnp.int32, (64, ROWS), 0) == 0, 1.0, 0.0)
         rt[slot, 1, 72:128, :] = jnp.zeros((56, ROWS), F32)
 
-    own_copies[0].wait()
-    own_copies[1].wait()
-    for leaf in range(2):
-        prep(leaf, 0, 256)
-
-    rows_mine = jnp.zeros((SKEL, WIDTH), F32)
-    for leaf in range(2):
-        chosen_rows = select[:, 256 * leaf:256 * leaf + 256]
-        rows_mine += dot_nn(chosen_rows, hi[leaf]) + dot_nn(chosen_rows, lo[leaf])
-    for q in range(4):
-        for h in range(2):
-            contr[q, h] = rows_mine[64 * q + 32 * h:64 * q + 32 * h + 32, :]
-    contr_msg = send(contr.at[:, other], contr_in, sib)
 
     def mask_row(entries):
         row = jnp.zeros((1, 128), F32)
@@ -225,7 +221,7 @@
     masks[0, 3:4, :] = mask_row([fupper_ref[0, e] for e in range(15)])
     masks[0, 4:8, :] = jnp.zeros((4, 128), F32)
     mask_msgs = [send(masks.at[0], masks.at[slot], device)
-                 for slot, device in ((1, sib), (2, chip(1, j)), (4, chip(3, j)))]
+                 for slot, device in ((1, sib), (2, to_after), (3, to_before))]
 
     def chip_sum(mine, incoming, total):
         for q in range(4):
@@ -293,13 +289,13 @@
     up_one = phase_one(up)
     send_bulk()
     weight_msgs = [send(rt.at[0, 1, 0:MSG], rt.at[slot, 1, 0:MSG], device)
-                   for slot, device in ((1, sib), (2, chip(1, j)), (4, chip(3, j)))]
+                   for slot, device in ((1, sib), (2, to_after), (3, to_before))]
 
     finish(sib_points)
     label_msgs[2].wait_recv()
     mask_msgs[0].wait_recv()
     for leaf in range(2):
-        prep(2 + leaf, 0, 256)
+        prep(2 + leaf)
 
     finish(up_one)
     up_two = phase_two(up)
@@ -312,17 +308,10 @@
     send_bulk()
     share.wait_recv()
 
-    def prep_upper(i, carry):
-        value = uq[i].reshape(64, WIDTH)
-        rows = pl.ds(pl.multiple_of(i * 64, 64), 64)
-        high, low = split(value)
-        uhi[rows, :] = high
-        ulo[rows, :] = low
-        norm = jnp.sum(value * value, axis=1, keepdims=True) * BETA
-        uncol[rows, :] = jnp.broadcast_to(norm, (64, 128))
-        return carry
-    lax.fori_loop(0, 4, prep_upper, 0)
-    k = affine((uhi[...], ulo[...], uncol[...]), as_sources([(0, 0, 256), (1, 0, 256)]))
+    value = uq[...].reshape(SKEL, WIDTH)
+    u_hi, u_lo = split(value)
+    u_col = jnp.broadcast_to(jnp.sum(value * value, axis=1, keepdims=True) * BETA, (SKEL, 128))
+    k = affine((u_hi, u_lo, u_col), as_sources([(0, 0, 256), (1, 0, 256)]))
     total = jnp.sum(k, axis=0, keepdims=True)
     shares = k * jnp.where(srow[0:1, :] > 0.0, 1.0 / total, 0.0)
     partial_sum = product_nt(shares, rt[0, 1])
@@ -332,17 +321,13 @@
     wp_msg = send(wp.at[:, other], wp_in, sib)
 
     def prep_up(q, m):
-        def body(n, carry):
-            value = up[q, m, n].reshape(64, WIDTH)
-            rows = pl.ds(pl.multiple_of((q * 4 + m) * 256 + n * 64, 64), 64)
-            high, low = split(value)
-            uphi[rows, :] = high
-            uplo[rows, :] = low
-            norm = jnp.sum(value * value, axis=1, keepdims=True) * BETA
-            uncol[pl.ds(pl.multiple_of(n * 64, 64), 64), :] = jnp.broadcast_to(norm, (64, 128))
-            return carry
-        lax.fori_loop(0, 4, body, 0)
-        upnrow[q * 4 + m] = jnp.transpose(uncol[...])[0:8, :]
+        value = up[q, m].reshape(256, WIDTH)
+        rows = pl.ds(pl.multiple_of((q * 4 + m) * 256, 256), 256)
+        high, low = split(value)
+        uphi[rows, :] = high
+        uplo[rows, :] = low
+        wide = jnp.broadcast_to(jnp.sum(value * value, axis=1, keepdims=True) * BETA, (256, 128))
+        upnrow[q * 4 + m] = jnp.transpose(wide)[0:8, :]
 
     def far_own(step):
         m0, m1 = majors(step)
@@ -360,11 +345,6 @@
     w_ones = round_one(wpart, wland1)
     send_bulk()
 
-    finish(label_msgs[:2] + mask_msgs[1:] + weight_msgs[1:])
-    forward = []
-    for slot in (2, 4):
-        forward += [send(rt.at[slot, :, 0:MSG], rt.at[slot + 1, :, 0:MSG], sib),
-                    send(masks.at[slot], masks.at[slot + 1], sib)]
     finish(w_ones)
     w_twos = round_two(wpart, wland1, wmid, wland2)
     send_bulk(len(CHUNKS) - len(bulk[1]))
@@ -386,25 +366,24 @@
 
     taken = [0]
 
-    def piece_arrives(leaf, first, size):
-        end = 256 * leaf + first + size
-        while taken[0] < len(CHUNKS) and sum(CHUNKS[:taken[0] + 1]) <= end:
+    def leaf_arrives(leaf):
+        while taken[0] < len(CHUNKS) and sum(CHUNKS[:taken[0] + 1]) <= 256 * leaf + 256:
             bulk[1][taken[0]].wait_recv()
             bulk[3][taken[0]].wait_recv()
             taken[0] += 1
-        rows = pl.ds(first, size)
-        return [send(pts.at[4 + 2 * leaf + side, rows], pts.at[8 + 2 * leaf + side, rows], sib)
-                for side in range(2)]
-
-    passed = piece_arrives(0, 0, 256)
-    for buffer in (4, 5):
-        prep(buffer, 0, 256)
-    near(0, 0, OWN, [(4, 0, 256), (5, 0, 256)], [(2, nodes[2], 0, 0, 256), (4, nodes[4], 0, 0, 256)])
-    finish(passed)
-    finish(forward)
-    for buffer in (8, 9):
-        prep(buffer, 0, 256)
-    near(0, 0, OWN, [(8, 0, 256), (9, 0, 256)], [(3, nodes[3], 0, 0, 256), (5, nodes[5], 0, 0, 256)])
+        for side in range(2):
+            prep(4 + 2 * leaf + side)
+
+    SIB = [(2, 0, 0, 256), (3, 1, 0, 256)]
+
+    def from_leaf(target, slot, targets, leaf):
+        near(target, slot, targets, [(4 + 2 * leaf, 0, 256), (5 + 2 * leaf, 0, 256)],
+             [(2, nodes[2], leaf, 0, 256), (3, nodes[3], leaf, 0, 256)])
+
+    finish(label_msgs[:2] + mask_msgs[1:] + weight_msgs[1:])
+    leaf_arrives(0)
+    from_leaf(0, 0, OWN, 0)
+    from_leaf(3, 1, SIB, 0)
 
     finish(up_two[2])
     up_share[2] = share_step(up, 2)
@@ -413,14 +392,11 @@
     finish(up_share[2])
     far_own(2)
 
-    def far_kernel(target_pieces, q, m):
-        return split(affine(as_targets(target_pieces), up_pair([(q, m), (q, m + 1)])))
-
-    for side, (leaf, q) in enumerate(((4, 1), (cross_leaf, 0))):
-        for m in (0, 2):
-            k_hi, k_lo = far_kernel([(leaf, 0, 256)], q, m)
-            kn_hi[side, m // 2] = k_hi
-            kn_lo[side, m // 2] = k_lo
+    def far_kernel(leaf, q):
+        return split(affine(as_targets([(leaf, 0, 256)]), up_pair([(q, m) for m in range(4)])))
+
+    for side in range(2):
+        kn_hi[side], kn_lo[side] = far_kernel(4 + side, 1 - side)
 
     for s in (1, 3, 2):
         finish(w_up_two[s])
@@ -432,46 +408,31 @@
         rhs = jnp.concatenate([up_rhs(0, 0, m0), up_rhs(0, 1, m1)], axis=0)
         acc[0] += product_nn(kf_hi[step], kf_lo[step], rhs)
 
-    def far_terms(slot, q, m):
-        return jnp.concatenate([up_rhs(slot, q, m), up_rhs(slot, q, m + 1)], axis=0)
-
-    for side, (slot, q) in enumerate(((2, 1), (cross_slot, 0))):
-        for m in (0, 2):
-            acc[1 + side, 0:256, :] += product_nn(kn_hi[side, m // 2], kn_lo[side, m // 2], far_terms(slot, q, m))
-
-    for first in (0, 128):
-        passed = piece_arrives(1, first, 128)
-        for buffer in (6, 7):
-            prep(buffer, first, 128)
-        finish(passed)
-        for buffer in (10, 11):
-            prep(buffer, first, 128)
-
-        def own_piece():
-            near(0, 0, OWN, [(b, first, 128) for b in (6, 7, 10, 11)],
-                 [(sl, nodes[sl], 1, first, 128) for sl in (2, 4, 3, 5)])
-
-        if first == 0:
-            own_piece()
-        for side, (slot, leaf, q) in enumerate(((2, 6, 1), (cross_slot, cross_leaf + 2, 0))):
-            for m in (0, 2):
-                k_hi, k_lo = far_kernel([(leaf, first, 128)], q, m)
-                acc[1 + side, 256 + first:384 + first, :] += product_nn(k_hi, k_lo, far_terms(slot, q, m))
-
-    sides = ((2, nodes[2], 4), (cross_slot, cross_node, cross_leaf))
+    def far_terms(side):
+        return jnp.concatenate([up_rhs(2 + side, 1 - side, m) for m in range(4)], axis=0)
+
+    for side in range(2):
+        acc[1 + side, 0:256, :] += product_nn(kn_hi[side], kn_lo[side], far_terms(side))
+
+    leaf_arrives(1)
     backs = []
     for side in range(2):
-        slot, _, leaf = sides[side]
-        from_slot, from_node, from_leaf = sides[1 - side]
-        near(1 + side, slot, [(leaf, 0, 0, 256), (leaf + 2, 1, 0, 256)],
-             [(from_leaf, 0, 256), (from_leaf + 2, 0, 256)],
-             [(from_slot, from_node, 0, 0, 256), (from_slot, from_node, 1, 0, 256)])
+        near(1 + side, 2 + side, [(4 + side, 0, 0, 256), (6 + side, 1, 0, 256)],
+             [(5 - side, 0, 256), (7 - side, 0, 256)],
+             [(3 - side, nodes[3 - side], 0, 0, 256), (3 - side, nodes[3 - side], 1, 0, 256)])
+        k_hi, k_lo = far_kernel(6 + side, 1 - side)
+        acc[1 + side, 256:512, :] += product_nn(k_hi, k_lo, far_terms(side))
         ret_out[side] = jnp.transpose(acc[1 + side])
         backs.append(send(ret_out.at[side, 0:MSG], ret_in.at[side, 0:MSG],
                           chip(3, j) if side == 0 else chip(1, crossed)))
-    own_piece()
-    finish(backs)
-    sums = jnp.transpose(acc[0])[0:MSG] + ret_in[0, 0:MSG] + ret_in[1, 0:MSG]
+    from_leaf(3, 1, SIB, 1)
+    ret_out[2] = jnp.transpose(acc[3])
+    backs.append(send(ret_out.at[2, 0:MSG], ret_in.at[2, 0:MSG], sib))
+    from_leaf(0, 0, OWN, 1)
+    sums = jnp.transpose(acc[0])[0:MSG]
+    for side in (2, 0, 1):
+        backs[side].wait_recv()
+        sums += ret_in[side, 0:MSG]
     out_ref[...] = sums[0:LABELS] / sums[LABELS:LABELS + 1]
 
     for copy in started:
@@ -491,13 +452,13 @@
         in_specs=[hbm, hbm, vmem, vmem, smem, smem, smem],
         out_specs=vmem,
         scratch_shapes=[
-            pltpu.VMEM((12, LEAF, WIDTH), F32),
-            pltpu.VMEM((12, LEAF, WIDTH), BF16),
-            pltpu.VMEM((12, LEAF, WIDTH), BF16),
-            pltpu.VMEM((12, LEAF, 128), F32),
-            pltpu.VMEM((12, 8, LEAF), F32),
-            pltpu.VMEM((6, 2, 128, ROWS), F32),
-            pltpu.VMEM((6, 8, 128), F32),
+            pltpu.VMEM((8, LEAF, WIDTH), F32),
+            pltpu.VMEM((8, LEAF, WIDTH), BF16),
+            pltpu.VMEM((8, LEAF, WIDTH), BF16),
+            pltpu.VMEM((8, LEAF, 128), F32),
+            pltpu.VMEM((8, 8, LEAF), F32),
+            pltpu.VMEM((4, 2, 128, ROWS), F32),
+            pltpu.VMEM((4, 8, 128), F32),
             pltpu.VMEM((ROWS, ROWS), F32),
             pltpu.VMEM((ROWS, 128), F32),
             pltpu.VMEM((8, ROWS), F32),
@@ -508,9 +469,6 @@
             pltpu.VMEM((2, 32, WIDTH), F32),
             pltpu.VMEM((2, 32, WIDTH), F32),
             pltpu.VMEM((4, 2, 32, WIDTH), F32),
-            pltpu.VMEM((SKEL, WIDTH), BF16),
-            pltpu.VMEM((SKEL, WIDTH), BF16),
-            pltpu.VMEM((SKEL, 128), F32),
             pltpu.VMEM((2, 4, 4, 2, 32, WIDTH), F32),
             pltpu.VMEM((2048, WIDTH), BF16),
             pltpu.VMEM((2048, WIDTH), BF16),
@@ -524,11 +482,11 @@
             pltpu.VMEM((2, 4, 4, 2, 32, 128), F32),
             pltpu.VMEM((4, ROWS, ROWS), BF16),
             pltpu.VMEM((4, ROWS, ROWS), BF16),
-            pltpu.VMEM((2, 2, LEAF, ROWS), BF16),
-            pltpu.VMEM((2, 2, LEAF, ROWS), BF16),
-            pltpu.VMEM((3, ROWS, 128), F32),
-            pltpu.VMEM((2, 128, ROWS), F32),
-            pltpu.VMEM((2, 128, ROWS), F32),
+            pltpu.VMEM((2, LEAF, 1024), BF16),
+            pltpu.VMEM((2, LEAF, 1024), BF16),
+            pltpu.VMEM((4, ROWS, 128), F32),
+            pltpu.VMEM((3, 128, ROWS), F32),
+            pltpu.VMEM((3, 128, ROWS), F32),
             pltpu.SemaphoreType.DMA((3,)),
             pltpu.SemaphoreType.DMA((N_COPIES,)),
             pltpu.SemaphoreType.DMA((N_COPIES,)),

time: 96.3 us -> 79.8 us (0.83)
  Pallas kernels: 94.6 us -> 77.9 us
    pallas_call x1, Pallas kernels: 94.6 us -> 77.9 us  [on_device(): pl.pallas_call(kernel, out_shape=jax.ShapeDtypeStruct((LABELS, ROWS), F32...]
where the time goes in v3:
time: 79.8 us; the launch traced here: 79.4 us
  Pallas kernels  77.9 us (98%)
  local copies, waits for them, and re-layouts  1.57 us (2%)
    pallas_call x1, Pallas kernels, on_device(): pl.pallas_call(kernel, out_shape=jax.ShapeDtypeStruct((LABELS, ROWS), F32...  77.9 us

profile of v3, /device:TPU:1, one launch (start us, length us, event | category | flops | bytes accessed | tf_op | source)
XLA Modules:
  0.0 79.4 jit_solution(800265778672047079)
XLA Ops:
  0.0 77.9 %shard_map.73 = f32[64,512]{1,0:T(8,128)} custom-call(f32[512,768]{1,0:T(8,128)} %x_ref.1, f32[64,512]{1,0:T(8,128)} %bitcast.3, s32[1,256]{1,0:T(1,128)} %skel_ref.1, s32[1,256]{1,0:T(1,128)} %urow_ref.1, s32[2,8]{1,0:T(2,128)} %near_ref.1, s32[1,7]{1,0:T(1,128)} %flocal_ref.1, s32[1,15]{1,0:T(1,128)} %fupper_ref.1), custom_call_target="tpu_custom_call" | custom-call | flops 19327352832 | bytes 2097152 | tf_op jit(solution)/shard_map/pallas_call | solution.py:449
  77.9 1.6 %copy.9 = f32[512,64]{0,1:T(8,128)} copy(f32[512,64]{0,1:T(8,128)} %bitcast.2) | data formatting | bytes 262144

commit v4 on v3

--- a/solution.py
+++ b/solution.py
@@ -12,7 +12,7 @@
 F32, BF16 = jnp.float32, jnp.bfloat16
 ROWS, WIDTH, LABELS, SKEL, LEAF = 512, 768, 64, 256, 256
 MSG = 72
-CHUNKS = (32, 32, 32, 32, 64, 64, 128, 128)
+CHUNKS = (32, 32, 32, 32, 64, 32, 32, 64, 64, 128)
 BETA = 25.0 * math.log2(math.e)
 
 
@@ -29,7 +29,8 @@
     return high, (value - high.astype(F32)).astype(BF16)
 
 
-def kernel(x_ref, lab_ref, skel_ref, urow_ref, near_ref, flocal_ref, fupper_ref, out_ref,
+def kernel(x_ref, lab_ref, skel_hbm, urow_hbm, near_hbm, flocal_hbm, fupper_hbm, out_ref,
+           skel_ref, urow_ref, near_ref, flocal_ref, fupper_ref,
            pts, hi, lo, ncol, nrow, rt, masks, kown, scol, srow,
            contr, contr_in, part, land1, mid, land2, uq,
            up, uphi, uplo, upnrow,
@@ -58,7 +59,10 @@
     own_copies = [pltpu.make_async_copy(x_ref.at[pl.ds(256 * leaf, 256)], pts.at[leaf], own_sem.at[leaf])
                   for leaf in range(2)]
     own_copies.append(pltpu.make_async_copy(lab_ref, rt.at[0, 0, 0:64], own_sem.at[2]))
-    for copy in own_copies:
+    small = ((skel_hbm, skel_ref), (urow_hbm, urow_ref), (near_hbm, near_ref),
+             (flocal_hbm, flocal_ref), (fupper_hbm, fupper_ref))
+    own_copies += [pltpu.make_async_copy(src, dst, own_sem.at[3 + at]) for at, (src, dst) in enumerate(small)]
+    for copy in own_copies[3:] + own_copies[:3]:
         copy.start()
 
     partners = [sib] + [chip(s, k) for s in (1, 3) for k in (j, other)]
@@ -67,6 +71,8 @@
     for partner in partners:
         pl.semaphore_signal(barrier, inc=1, device_id=partner, device_id_type=MESH)
 
+    own_copies[3].wait()
+    own_copies[4].wait()
     skel_t = jnp.where(lax.broadcasted_iota(jnp.int32, (ROWS, SKEL), 0) == skel_ref[...], 1.0, 0.0)
     scol[...] = jnp.broadcast_to(jnp.max(skel_t, axis=1, keepdims=True), (ROWS, 128))
     skel = jnp.transpose(skel_t)
@@ -209,6 +215,8 @@
         rt[slot, 1, 72:128, :] = jnp.zeros((56, ROWS), F32)
 
 
+    for copy in own_copies[5:]:
+        copy.wait()
     def mask_row(entries):
         row = jnp.zeros((1, 128), F32)
         for entry in entries:
@@ -276,7 +284,15 @@
 
     def phase_two(buffer):
         return {s: [send(buffer.at[0, z, :, j], buffer.at[0, z, :, j], z_peer(s)),
-                    send(buffer.at[1, y, :, j], buffer.at[1, y, :, j], y_peer(s))] for s in (1, 3, 2)}
+                    send(buffer.at[1, y, :, j], buffer.at[1, y, :, j], y_peer(s))] for s in (1, 3)}
+
+    def pass_on(buffer):
+        copies = []
+        for step, rows in ((1, slice(0, 2)), (3, slice(2, 4))):
+            m0, m1 = majors(step)
+            copies += [send(buffer.at[0, m0, rows, j], buffer.at[0, m0, rows, j], z_peer(step)),
+                       send(buffer.at[1, m1, rows, j], buffer.at[1, m1, rows, j], y_peer(step))]
+        return copies
 
     def majors(step):
         return lax.rem(z + 4 - step, 4), lax.rem(y + 4 - step, 4)
@@ -290,6 +306,8 @@
     send_bulk()
     weight_msgs = [send(rt.at[0, 1, 0:MSG], rt.at[slot, 1, 0:MSG], device)
                    for slot, device in ((1, sib), (2, to_after), (3, to_before))]
+
+    send_bulk()
 
     finish(sib_points)
     label_msgs[2].wait_recv()
@@ -337,32 +355,20 @@
         kf_hi[step] = k_hi
         kf_lo[step] = k_lo
 
-    finish(up_share[0])
-    far_own(0)
-
     wp_msg.wait_recv()
     chip_sum(wp, wp_in, wpart)
     w_ones = round_one(wpart, wland1)
     send_bulk()
-
+    finish(up_share[0])
+    far_own(0)
     finish(w_ones)
     w_twos = round_two(wpart, wland1, wmid, wland2)
     send_bulk(len(CHUNKS) - len(bulk[1]))
-
-    finish(up_two[1])
-    up_share[1] = share_step(up, 1)
-    finish(up_two[3])
-    up_share[3] = share_step(up, 3)
-
-    finish(w_twos)
-    upw[0, z, y, j] = wmid[0] + wland2[0]
-    upw[1, y, z, j] = wmid[1] + wland2[1]
-    w_up_one = phase_one(upw)
-
-    finish(up_share[1])
-    far_own(1)
-    finish(up_share[3])
-    far_own(3)
+    for step in (1, 3):
+        finish(up_two[step])
+    up_two[2] = pass_on(up)
+    for step in (1, 3):
+        up_share[step] = share_step(up, step)
 
     taken = [0]
 
@@ -382,15 +388,28 @@
 
     finish(label_msgs[:2] + mask_msgs[1:] + weight_msgs[1:])
     leaf_arrives(0)
+    from_leaf(3, 1, SIB, 0)
+    finish(w_twos)
+    upw[0, z, y, j] = wmid[0] + wland2[0]
+    upw[1, y, z, j] = wmid[1] + wland2[1]
+    w_up_one = phase_one(upw)
     from_leaf(0, 0, OWN, 0)
-    from_leaf(3, 1, SIB, 0)
 
     finish(up_two[2])
     up_share[2] = share_step(up, 2)
+    finish(up_share[1])
+    far_own(1)
     finish(w_up_one)
     w_up_two = phase_two(upw)
+    finish(up_share[3])
+    far_own(3)
+    for step in (1, 3):
+        finish(w_up_two[step])
+    w_pass = pass_on(upw)
     finish(up_share[2])
     far_own(2)
+    finish(w_pass)
+    w_share = [send(upw.at[:, :, :, j], upw.at[:, :, :, j], sib)]
 
     def far_kernel(leaf, q):
         return split(affine(as_targets([(leaf, 0, 256)]), up_pair([(q, m) for m in range(4)])))
@@ -398,9 +417,6 @@
     for side in range(2):
         kn_hi[side], kn_lo[side] = far_kernel(4 + side, 1 - side)
 
-    for s in (1, 3, 2):
-        finish(w_up_two[s])
-    w_share = [send(upw.at[:, :, :, j], upw.at[:, :, :, j], sib)]
     finish(w_share)
 
     for step in range(4):
@@ -415,14 +431,26 @@
         acc[1 + side, 0:256, :] += product_nn(kn_hi[side], kn_lo[side], far_terms(side))
 
     leaf_arrives(1)
+    both = [[(4 + side, 0, 256), (6 + side, 0, 256)] for side in range(2)]
+    terms = [[(2 + side, nodes[2 + side], leaf, 0, 256) for leaf in range(2)] for side in range(2)]
+    k_hi, k_lo = split(affine(as_targets(both[0]), as_sources(both[1])))
+    turned = []
+    for t in range(2):
+        cols = slice(256 * t, 256 * t + 256)
+        r_hi, r_lo = split(near_rhs(3, t, terms[0]))
+        two = dot_nn(jnp.concatenate([r_hi, r_lo], axis=0), k_hi[:, cols])
+        turned.append(two[:128] + two[128:] + dot_nn(r_hi, k_lo[:, cols]))
+        rows = slice(256 * t, 256 * t + 256)
+        r_hi, r_lo = split(near_rhs(2, t, terms[1]))
+        two = dot_nt(k_hi[rows], jnp.concatenate([r_hi, r_lo], axis=0))
+        acc[1, rows, :] += two[:, :128] + two[:, 128:] + dot_nt(k_lo[rows], r_hi)
+    ret_out[1] = jnp.concatenate(turned, axis=1)
     backs = []
     for side in range(2):
-        near(1 + side, 2 + side, [(4 + side, 0, 0, 256), (6 + side, 1, 0, 256)],
-             [(5 - side, 0, 256), (7 - side, 0, 256)],
-             [(3 - side, nodes[3 - side], 0, 0, 256), (3 - side, nodes[3 - side], 1, 0, 256)])
-        k_hi, k_lo = far_kernel(6 + side, 1 - side)
-        acc[1 + side, 256:512, :] += product_nn(k_hi, k_lo, far_terms(side))
-        ret_out[side] = jnp.transpose(acc[1 + side])
+        f_hi, f_lo = far_kernel(6 + side, 1 - side)
+        acc[1 + side, 256:512, :] += product_nn(f_hi, f_lo, far_terms(side))
+        done = jnp.transpose(acc[1 + side])
+        ret_out[side] = done if side == 0 else ret_out[1] + done
         backs.append(send(ret_out.at[side, 0:MSG], ret_in.at[side, 0:MSG],
                           chip(3, j) if side == 0 else chip(1, crossed)))
     from_leaf(3, 1, SIB, 1)
@@ -444,14 +472,18 @@
 
 def on_device(points, labels, skeleton_rows, upper_rows, near_list, far_local, far_upper):
     vmem = pl.BlockSpec(memory_space=pltpu.VMEM)
-    smem = pl.BlockSpec(memory_space=pltpu.SMEM)
     hbm = pl.BlockSpec(memory_space=pl.ANY)
     result = pl.pallas_call(
         kernel,
         out_shape=jax.ShapeDtypeStruct((LABELS, ROWS), F32),
-        in_specs=[hbm, hbm, vmem, vmem, smem, smem, smem],
+        in_specs=[hbm] * 7,
         out_specs=vmem,
         scratch_shapes=[
+            pltpu.VMEM(skeleton_rows.shape, jnp.int32),
+            pltpu.VMEM(upper_rows.shape, jnp.int32),
+            pltpu.SMEM(near_list.shape, jnp.int32),
+            pltpu.SMEM(far_local.shape, jnp.int32),
+            pltpu.SMEM(far_upper.shape, jnp.int32),
             pltpu.VMEM((8, LEAF, WIDTH), F32),
             pltpu.VMEM((8, LEAF, WIDTH), BF16),
             pltpu.VMEM((8, LEAF, WIDTH), BF16),
@@ -487,7 +519,7 @@
             pltpu.VMEM((4, ROWS, 128), F32),
             pltpu.VMEM((3, 128, ROWS), F32),
             pltpu.VMEM((3, 128, ROWS), F32),
-            pltpu.SemaphoreType.DMA((3,)),
+            pltpu.SemaphoreType.DMA((8,)),
             pltpu.SemaphoreType.DMA((N_COPIES,)),
             pltpu.SemaphoreType.DMA((N_COPIES,)),
         ],

time: 79.8 us -> 74.8 us (0.937)
  Pallas kernels: 77.9 us -> 73 us
    pallas_call x1, Pallas kernels: 77.9 us -> 73 us  [on_device(): pl.pallas_call(kernel, out_shape=jax.ShapeDtypeStruct((LABELS, ROWS), F32...]
where the time goes in v4:
time: 74.8 us; the launch traced here: 74.6 us
  Pallas kernels  73 us (98%)
  local copies, waits for them, and re-layouts  1.57 us (2%)
    pallas_call x1, Pallas kernels, on_device(): pl.pallas_call(kernel, out_shape=jax.ShapeDtypeStruct((LABELS, ROWS), F32...  73 us
    unnamed x1, local copies, waits for them, and re-layouts  1.57 us

profile of v4, /device:TPU:1, one launch (start us, length us, event | category | flops | bytes accessed | tf_op | source)
XLA Modules:
  0.0 74.6 jit_solution(1473396822661222372)
XLA Ops:
  0.0 73.0 %shard_map.73 = f32[64,512]{1,0:T(8,128)} custom-call(f32[512,768]{1,0:T(8,128)} %x_ref.1, f32[64,512]{1,0:T(8,128)} %bitcast.3, s32[1,256]{1,0:T(1,128)} %skel_hbm.1, s32[1,256]{1,0:T(1,128)} %urow_hbm.1, s32[2,8]{1,0:T(2,128)} %near_hbm.1, s32[1,7]{1,0:T(1,128)} %flocal_hbm.1, s32[1,15]{1,0:T(1,128)} %fupper_hbm.1), custom_call_target="tpu_custom_call" | custom-call | flops 19327352832 | bytes 2097152 | tf_op jit(solution)/shard_map/pallas_call | solution.py:476
  73.1 1.6 %copy.9 = f32[512,64]{0,1:T(8,128)} copy(f32[512,64]{0,1:T(8,128)} %bitcast.2) | data formatting | bytes 262144

commit v5 on v4

--- a/solution.py
+++ b/solution.py
@@ -12,7 +12,7 @@
 F32, BF16 = jnp.float32, jnp.bfloat16
 ROWS, WIDTH, LABELS, SKEL, LEAF = 512, 768, 64, 256, 256
 MSG = 72
-CHUNKS = (32, 32, 32, 32, 64, 32, 32, 64, 64, 128)
+CHUNKS = (32, 32, 32, 32, 48, 32, 48, 64, 64, 128)
 BETA = 25.0 * math.log2(math.e)
 
 

time: 74.8 us -> 74.5 us (level)
  no operation moved by 1% of the time
where the time goes in v5:
time: 74.5 us; the launch traced here: 74.3 us
  Pallas kernels  72.7 us (98%)
  local copies, waits for them, and re-layouts  1.57 us (2%)
    pallas_call x1, Pallas kernels, on_device(): pl.pallas_call(kernel, out_shape=jax.ShapeDtypeStruct((LABELS, ROWS), F32...  72.7 us
    unnamed x1, local copies, waits for them, and re-layouts  1.57 us

profile of v5, /device:TPU:1, one launch (start us, length us, event | category | flops | bytes accessed | tf_op | source)
XLA Modules:
  0.0 74.3 jit_solution(1217338246310104538)
XLA Ops:
  0.0 72.7 %shard_map.73 = f32[64,512]{1,0:T(8,128)} custom-call(f32[512,768]{1,0:T(8,128)} %x_ref.1, f32[64,512]{1,0:T(8,128)} %bitcast.3, s32[1,256]{1,0:T(1,128)} %skel_hbm.1, s32[1,256]{1,0:T(1,128)} %urow_hbm.1, s32[2,8]{1,0:T(2,128)} %near_hbm.1, s32[1,7]{1,0:T(1,128)} %flocal_hbm.1, s32[1,15]{1,0:T(1,128)} %fupper_hbm.1), custom_call_target="tpu_custom_call" | custom-call | flops 19327352832 | bytes 2097152 | tf_op jit(solution)/shard_map/pallas_call | solution.py:476
  72.7 1.6 %copy.9 = f32[512,64]{0,1:T(8,128)} copy(f32[512,64]{0,1:T(8,128)} %bitcast.2) | data formatting | bytes 262144
